TPU v7x, 32 devices: a whole 2x2x4 slice. The times are simulated.
32 devices in a mesh: gx: 8 (over z, y), gy: 4 (over x, core).
Axes of the slice: x: 2, y: 2, z: 4, core: 2. Of those that a mesh axis runs over, the one named last changes fastest.
Arguments:
- tile_sums: bfloat16 [1024, 5, 8192], P(('gx', 'gy')), may hold values from -180 to 180
- tile_dest: int32 [1024], P(('gx', 'gy')), may hold values from 0 to 31, as said below
- tile_place: int32 [1024], P(('gx', 'gy')), may hold values from 0 to 15
- tile_count: int32 [32], P(('gx', 'gy')), may hold values from 16 to 32, as said below
Outputs:
- smoothed: float32 [5, 8, 512, 1024], P(None, 'gx', 'gy')
Inputs may be any that keep to these rules, and one draw needn't show every extreme that they name: `tile_dest`: each DEM device's 32 records name every filter device exactly once. Only the first tile_count[d] slots of device d are live; some device has all 32 live and some has half.
All inputs are finite; a program needn't handle non-finite values.
Results may differ from a plain program's by a relative error of at most 0.0003.
Values may be sent and summed in bfloat16 or wider, within the bound.
A program may use at most 192 MiB of HBM per device.

v0:
```python
import math

import jax
import jax.numpy as jnp
from jax import lax
from jax.sharding import PartitionSpec as P

TE = 32
BX = 4
BY = 4
RADIUS = 4


def padded_2(cells, sides, width):
    for axis, dim in sides:
        count = lax.axis_size(axis)
        ends = count - 1
        head = lax.slice_in_dim(cells, 0, width, axis=dim)
        tail = lax.slice_in_dim(cells, cells.shape[dim] - width, cells.shape[dim], axis=dim)
        cells = jnp.concatenate(
            [
                lax.ppermute(tail, axis, [(i, (i + 1) % count) for i in range(ends)]),
                cells,
                lax.ppermute(head, axis, [((i + 1) % count, i) for i in range(ends)]),
            ],
            axis=dim,
        )
    return cells


def gauss_taps():
    spread = RADIUS * 5.0 / 16.0
    raw_taps = [
        math.exp(-(offset * offset) / (2.0 * spread * spread))
        for offset in range(-RADIUS, RADIUS + 1)
    ]
    total_weight = sum(raw_taps)
    return [value / total_weight for value in raw_taps]


def zero_pad(field, axis):
    widths = [(0, 0)] * field.ndim
    widths[axis] = (RADIUS, RADIUS)
    return jnp.pad(field, widths)


def smooth_axis(padded, axis, taps, length):
    result = taps[0] * lax.slice_in_dim(padded, 0, length, axis=axis)
    for offset in range(1, len(taps)):
        result = result + taps[offset] * lax.slice_in_dim(
            padded, offset, offset + length, axis=axis
        )
    return result


def local(tile_sums, tile_dest, tile_place, tile_count):
    slot_count = tile_sums.shape[0]
    fields = tile_sums.shape[1]
    cells = tile_sums.shape[2]
    planes = cells // (TE * TE)
    across = lax.axis_size("gx")
    column_count = lax.axis_size("gy")
    peer_count = across * column_count
    is_live = jnp.arange(slot_count, dtype=jnp.int32) < tile_count[0]
    targets = jnp.arange(peer_count, dtype=jnp.int32)
    chosen = (tile_dest[None, :] == targets[:, None]) & is_live[None, :]
    outgoing = jnp.dot(
        chosen.astype(jnp.bfloat16),
        tile_sums.reshape(slot_count, fields * cells),
        preferred_element_type=jnp.float32,
    ).astype(jnp.bfloat16)
    out_place = jnp.sum(jnp.where(chosen, tile_place[None, :] + 1, 0), axis=1) - 1
    incoming, in_place = (
        lax.all_to_all(outgoing, ("gx", "gy"), split_axis=0, concat_axis=0, tiled=True),
        lax.all_to_all(out_place[:, None], ("gx", "gy"), split_axis=0, concat_axis=0, tiled=True),
    )
    in_place = in_place.reshape(peer_count)
    local_ids = jnp.arange(BX * BY, dtype=jnp.int32)
    landing = (in_place[None, :] == local_ids[:, None]).astype(jnp.bfloat16)
    deposited = jnp.dot(landing, incoming, preferred_element_type=jnp.float32)
    deposited = deposited.reshape(BY, BX, fields, planes, TE, TE).transpose(2, 3, 0, 4, 1, 5)
    deposited = deposited.reshape(fields, planes, BY * TE, BX * TE)
    taps = gauss_taps()
    height = BY * TE
    width = BX * TE
    padded = padded_2(deposited, (("gx", 3), ("gy", 2)), RADIUS)
    along_x = smooth_axis(padded, 3, taps, width)
    along_y = smooth_axis(along_x, 2, taps, height)
    along_z = smooth_axis(zero_pad(along_y, 1), 1, taps, planes)
    return lax.all_to_all(along_z, "gx", split_axis=1, concat_axis=3, tiled=True)


def solution(mesh):
    return jax.shard_map(
        local,
        mesh=mesh,
        in_specs=(P(("gx", "gy"), None, None), P(("gx", "gy")), P(("gx", "gy")), P(("gx", "gy"))),
        out_specs=P(None, "gx", "gy", None),
        check_vma=False,
    )
```

profile of v0, /device:TPU:1, one launch (start us, length us, event | category | flops | bytes accessed | tf_op | source)
XLA Modules:
  0.0 277.8 jit_solution(2134256432638163582)
XLA Ops:
  2.8 7.1 %all-to-all-start = ((s32[32,1,1]{2,1,0:T(1,128)}), s32[32,1,1]{2,1,0:T(1,128)S(1)}, u32[]{:S(2)}, u32[]{:S(2)}) async-start(s32[32,1,1]{2,1,0:T(1,128)} %copy.38), calls=%async_computation | async-start | bytes 32768 | tf_op jit(solution)/shard_map/all_to_all | solution.py:75
  11.9 2.3 fusion
  14.7 4.4 %reduce.1 = bf16[32,40960]{1,0:T(8,128)(2,1)S(1)} reduce(bf16[32,1,40960]{2,0,1:T(8,128)(2,1)} %fusion, bf16[]{:T(256)} %broadcast.93), dimensions={1}, to_apply=%copy.40.reduce_sub_computation | reduce | bytes 5242882 | tf_op jit(solution)/shard_map/all_to_all | solution.py:74
  19.1 3.2 %reshape.54 = bf16[32,2,20480]{2,1,0:T(2,128)(2,1)} reshape(bf16[32,40960]{1,0:T(8,128)(2,1)S(1)} %reduce.1) | data formatting | bytes 5242880
  22.3 5.8 %all-to-all-start.1 = ((bf16[32,2,20480]{2,1,0:T(2,128)(2,1)}), bf16[32,2,20480]{2,1,0:T(2,128)(2,1)S(1)}, u32[]{:S(2)}, u32[]{:S(2)}) async-start(bf16[32,2,20480]{2,1,0:T(2,128)(2,1)} %reshape.54), calls=%async_computation.1 | async-start | bytes 5242880 | tf_op jit(solution)/shard_map/all_to_all | solution.py:74
  28.8 59.0 %all-to-all-done.1 = bf16[32,2,20480]{2,1,0:T(2,128)(2,1)S(1)} async-done(((bf16[32,2,20480]{2,1,0:T(2,128)(2,1)}), bf16[32,2,20480]{2,1,0:T(2,128)(2,1)S(1)}, u32[]{:S(2)}, u32[]{:S(2)}) %all-to-all-start.1) | async-done | bytes 2621472 | tf_op jit(solution)/shard_map/all_to_all | solution.py:74
  87.8 7.2 %reshape.55 = bf16[32,1,40960]{2,1,0:T(2,128)(2,1)} reshape(bf16[32,2,20480]{2,1,0:T(2,128)(2,1)S(1)} %all-to-all-done.1) | data formatting | bytes 5242880
  95.0 15.4 %copy.52 = bf16[32,1,40960]{0,2,1:T(8,128)(2,1)} copy(bf16[32,1,40960]{2,1,0:T(2,128)(2,1)} %reshape.55) | data formatting | bytes 5242880 | tf_op jit(solution)/shard_map/dot_general | solution.py:80
  110.4 21.4 %convolution_bitcast_fusion = f32[5,8,4,32,4,32]{5,4,3,1,0,2:T(4,128)} fusion(bf16[5,8,32,32,32,1]{4,3,2,1,0,5:T(8,128)(2,1)} %bitcast.30, s32[4,4]{1,0:T(4,128)S(1)} %multiply_add_fusion, s32[32]{0:T(128)S(1)} %reduce), kind=kOutput, calls=%fused_computation.11 | convolution fusion | flops 41943552 | bytes 5243072 | tf_op jit(solution)/shard_map/dot_general | solution.py:80
  131.8 12.1 %copy.42 = f32[5,8,4,32,4,32]{5,4,3,2,1,0:T(4,128)} copy(f32[5,8,4,32,4,32]{5,4,3,1,0,2:T(4,128)} %convolution_bitcast_fusion) | data formatting | bytes 5242880 | tf_op jit(solution)/shard_map/transpose | solution.py:81
  144.0 7.8 %reshape.50 = f32[5,8,128,128]{3,2,1,0:T(8,128)S(1)} reshape(f32[5,8,4,32,4,32]{5,4,3,2,1,0:T(4,128)} %copy.42) | data formatting | bytes 5242880 | tf_op jit(solution)/shard_map/reshape | solution.py:82
  151.8 3.3 %fusion.41 = (f32[5,8,128,4]{3,2,1,0:T(8,128)}, f32[5,8,128,4]{3,2,1,0:T(8,128)}) fusion(f32[5,8,128,128]{3,2,1,0:T(8,128)S(1)} %reshape.50), kind=kLoop, calls=%fused_computation.78 | loop fusion | bytes 327680 | tf_op jit(solution)/shard_map/slice | solution.py:19
  155.1 2.5 copy.43
  157.6 2.8 %collective-permute-start = (f32[5,8,128,4]{2,1,3,0:T(8,128)S(1)}, f32[5,8,128,4]{2,1,3,0:T(8,128)S(1)}, u32[]{:S(2)}, u32[]{:S(2)}) collective-permute-start(f32[5,8,128,4]{2,1,3,0:T(8,128)S(1)} %copy.43), channel_id=1, source_target_pairs={{0,4},{4,8},{8,12},{12,16},{16,20},{20,24},{24,28},{1,5},{5,9},{9,... | collective-permute-start | bytes 245768 | tf_op jit(solution)/shard_map/ppermute | solution.py:22
  160.4 2.5 copy.44
  164.4 2.3 copy.45
  168.1 2.3 copy.46
  172.0 5.5 %collective-permute-start.2 = (f32[5,8,4,136]{3,2,1,0:T(4,128)S(1)}, f32[5,8,4,136]{3,2,1,0:T(4,128)S(1)}, u32[]{:S(2)}, u32[]{:S(2)}) collective-permute-start(f32[5,8,4,136]{3,2,1,0:T(4,128)S(1)} %get-tuple-element.5), channel_id=1, source_target_pairs={{0,1},{1,2},{2,3},{4,5},{5,6},{6,7},{8,9},{9,10},{10,11},{12,13},{... | collective-permute-start | bytes 261128 | tf_op jit(solution)/shard_map/ppermute | solution.py:22
  179.8 4.4 %collective-permute-done.3 = f32[5,8,4,136]{3,2,1,0:T(4,128)S(1)} collective-permute-done((f32[5,8,4,136]{3,2,1,0:T(4,128)S(1)}, f32[5,8,4,136]{3,2,1,0:T(4,128)S(1)}, u32[]{:S(2)}, u32[]{:S(2)}) %collective-permute-start.3) | collective-permute-done | bytes 87072 | tf_op jit(solution)/shard_map/ppermute | solution.py:24
  184.2 4.2 %pad_maximum_fusion = f32[5,8,136,136]{3,2,1,0:T(8,128)} fusion(f32[5,8,4,136]{3,2,1,0:T(4,128)S(1)} %collective-permute-done.3, f32[5,8,128,4]{3,2,1,0:T(8,128)S(1)} %copy-done.1, f32[5,8,128,128]{3,2,1,0:T(8,128)S(1)} %reshape.50, f32[5,8,128,4]{3,2,1,0:T(8,128)S(1)} %copy-done, f32[5,8,4,136]{3,2,1,0:T(4,128)S(1)} %collective-permute-done.2), kind=kLoop, calls=%fused_computation.10 | loop fusion | flops 2959360 | bytes 5918720 | tf_op jit(solution)/shard_map/concatenate | solution.py:20
  188.4 18.6 %fusion.1 = f32[5,8,136,128]{3,2,1,0:T(8,128)S(1)} fusion(f32[5,8,136,136]{3,2,1,0:T(8,128)} %pad_maximum_fusion), kind=kLoop, calls=%fused_computation.13 | loop fusion | flops 11837440 | bytes 27852800 | tf_op jit(solution)/shard_map/add | solution.py:50
  207.1 2.7 fusion.25
  212.1 60.4 %all_to_all.36 = f32[5,8,128,128]{3,2,0,1:T(8,128)S(1)} all-to-all(f32[5,8,128,128]{3,2,0,1:T(8,128)S(1)} %copy.47), channel_id=1, replica_groups=mesh['gx'=8,'gy'=4] {'gx'}, dimensions={1} | all-to-all | bytes 5242880 | tf_op jit(solution)/shard_map/all_to_all | solution.py:90
  274.6 3.2 %copy.49 = f32[5,1,128,1024]{3,2,1,0:T(8,128)} copy(f32[5,1,128,1024]{2,3,0,1:T(8,128)} %bitcast.32) | data formatting | bytes 5242880 | tf_op jit(solution)/shard_map/all_to_all | solution.py:90
  (25 shorter events, 16.3 us)
Async XLA Ops:
  2.8 19.5 %all-to-all-start = ((s32[32,1,1]{2,1,0:T(1,128)}), s32[32,1,1]{2,1,0:T(1,128)S(1)}, u32[]{:S(2)}, u32[]{:S(2)}) async-start(s32[32,1,1]{2,1,0:T(1,128)} %copy.38), calls=%async_computation | async-start | bytes 32768 | tf_op jit(solution)/shard_map/all_to_all | solution.py:75
  9.9 2.0 copy-start.2
  22.3 65.5 %all-to-all-start.1 = ((bf16[32,2,20480]{2,1,0:T(2,128)(2,1)}), bf16[32,2,20480]{2,1,0:T(2,128)(2,1)S(1)}, u32[]{:S(2)}, u32[]{:S(2)}) async-start(bf16[32,2,20480]{2,1,0:T(2,128)(2,1)} %reshape.54), calls=%async_computation.1 | async-start | bytes 5242880 | tf_op jit(solution)/shard_map/all_to_all | solution.py:74
  157.6 6.8 %collective-permute-start = (f32[5,8,128,4]{2,1,3,0:T(8,128)S(1)}, f32[5,8,128,4]{2,1,3,0:T(8,128)S(1)}, u32[]{:S(2)}, u32[]{:S(2)}) collective-permute-start(f32[5,8,128,4]{2,1,3,0:T(8,128)S(1)} %copy.43), channel_id=1, source_target_pairs={{0,4},{4,8},{8,12},{12,16},{16,20},{20,24},{24,28},{1,5},{5,9},{9,... | collective-permute-start | bytes 245768 | tf_op jit(solution)/shard_map/ppermute | solution.py:22
  162.9 5.2 %collective-permute-start.1 = (f32[5,8,128,4]{2,1,3,0:T(8,128)S(1)}, f32[5,8,128,4]{2,1,3,0:T(8,128)S(1)}, u32[]{:S(2)}, u32[]{:S(2)}) collective-permute-start(f32[5,8,128,4]{2,1,3,0:T(8,128)S(1)} %copy.44), channel_id=1, source_target_pairs={{4,0},{8,4},{12,8},{16,12},{20,16},{24,20},{28,24},{5,1},{9,5},{13... | collective-permute-start | bytes 245768 | tf_op jit(solution)/shard_map/ppermute | solution.py:24
  170.4 13.8 %copy-start = (f32[5,8,128,4]{3,2,1,0:T(8,128)S(1)}, f32[5,8,128,4]{3,2,1,0:T(8,128)}, u32[]{:S(2)}) copy-start(f32[5,8,128,4]{3,2,1,0:T(8,128)} %copy.45) | copy-start | bytes 245764
  170.4 13.8 %copy-start.1 = (f32[5,8,128,4]{3,2,1,0:T(8,128)S(1)}, f32[5,8,128,4]{3,2,1,0:T(8,128)}, u32[]{:S(2)}) copy-start(f32[5,8,128,4]{3,2,1,0:T(8,128)} %copy.46) | copy-start | bytes 245764
  172.0 7.7 %collective-permute-start.2 = (f32[5,8,4,136]{3,2,1,0:T(4,128)S(1)}, f32[5,8,4,136]{3,2,1,0:T(4,128)S(1)}, u32[]{:S(2)}, u32[]{:S(2)}) collective-permute-start(f32[5,8,4,136]{3,2,1,0:T(4,128)S(1)} %get-tuple-element.5), channel_id=1, source_target_pairs={{0,1},{1,2},{2,3},{4,5},{5,6},{6,7},{8,9},{9,10},{10,11},{12,13},{... | collective-permute-start | bytes 261128 | tf_op jit(solution)/shard_map/ppermute | solution.py:22
  177.5 6.6 %collective-permute-start.3 = (f32[5,8,4,136]{3,2,1,0:T(4,128)S(1)}, f32[5,8,4,136]{3,2,1,0:T(4,128)S(1)}, u32[]{:S(2)}, u32[]{:S(2)}) collective-permute-start(f32[5,8,4,136]{3,2,1,0:T(4,128)S(1)} %get-tuple-element.6), channel_id=1, source_target_pairs={{1,0},{2,1},{3,2},{5,4},{6,5},{7,6},{9,8},{10,9},{11,10},{13,12},{... | collective-permute-start | bytes 261128 | tf_op jit(solution)/shard_map/ppermute | solution.py:24
where the time goes:
time: 279 us; the launch traced here: 278 us
  local copies, waits for them, and re-layouts  67.3 us (24%)
  waiting for transfers between devices  65 us (23%)
  blocking collectives  60.4 us (22%)
  other arithmetic  35.8 us (13%)
  starting transfers between devices  24.6 us (9%)
  matrix products  23.8 us (9%)
    all_to_all x1, blocking collectives, local(): lax.all_to_all(along_z, 'gx', split_axis=1, concat_axis=3, tiled=True)  60.4 us
    all_to_all x1, waiting for transfers between devices, local(): lax.all_to_all(outgoing, ('gx', 'gy'), split_axis=0, concat_axis=0, tiled...  59 us
    add x3, other arithmetic, smooth_axis(): result + taps[offset] * lax.slice_in_dim(padded, offset, offset + length,...  23.5 us
    dot_general x1, matrix products, local(): deposited = jnp.dot(landing, incoming, preferred_element_type=jnp.float32)  21.4 us
    dot_general x1, local copies, waits for them, and re-layouts, local(): deposited = jnp.dot(landing, incoming, preferred_element_type=jnp.float32)  15.4 us
    transpose x1, local copies, waits for them, and re-layouts, local(): deposited.reshape(BY, BX, fields, planes, TE, TE)  12.1 us
    unnamed x8, local copies, waits for them, and re-layouts  10.4 us
    ppermute x2, starting transfers between devices, padded_2(): lax.ppermute(tail, axis, [(i, (i + 1) % count) for i in range(ends)])  8.28 us
  transfers between devices with their start and end apart: 6, of which 4 were waited for; matrix products, arithmetic and copies ran while one was open for 6% of the time, Pallas kernels for 0%

commit v1 on v0

v1 whole, which is shorter than its diff:
```python
import functools
import math

import jax
import jax.numpy as jnp
from jax import lax
from jax.experimental import pallas as pl
from jax.experimental.pallas import tpu as pltpu
from jax.sharding import PartitionSpec as P

TE = 32
BX = 4
BY = 4
RADIUS = 4
TILES = BX * BY
AREA = TE * TE
LANES = 128
ROWS = 16
VMEM_BYTES = 58 * 1024 * 1024


def gauss_taps():
    spread = RADIUS * 5.0 / 16.0
    raw_taps = [
        math.exp(-(offset * offset) / (2.0 * spread * spread))
        for offset in range(-RADIUS, RADIUS + 1)
    ]
    total_weight = sum(raw_taps)
    return [value / total_weight for value in raw_taps]


TAPS = gauss_taps()[RADIUS:]


def filter_list(values, first, count):
    products = {}
    results = []
    for k in range(count):
        total = None
        for j, value in enumerate(values):
            reach = abs(first + j - k)
            if reach > RADIUS:
                continue
            if (j, reach) not in products:
                products[j, reach] = value * TAPS[reach]
            term = products[j, reach]
            total = term if total is None else total + term
        results.append(total)
    return results


def encode_kernel(across, down, planes, sums_ref, dest_ref, place_ref, count_ref, send_ref, picked, smoothed, head):
    fields, slots, cells = sums_ref.shape
    parts = ROWS // across
    width = AREA // parts
    peers = across * down
    row = lax.broadcasted_iota(jnp.int32, (peers, slots), 0)
    slot = lax.broadcasted_iota(jnp.int32, (peers, slots), 1)
    target = (row % across) * down + row // across
    chosen = (dest_ref[...] == target) & (slot < count_ref[...])
    pick = jnp.where(chosen, 1.0, 0.0).astype(jnp.bfloat16)
    place = jnp.sum(jnp.where(chosen, place_ref[...] + 1, 0), axis=1, keepdims=True) - 1
    lane = lax.broadcasted_iota(jnp.int32, (across, LANES), 1)
    for column in range(down):
        start = jnp.where(lane == fields, place[column * across : (column + 1) * across], 0)
        for k in range(planes):
            head[k * down + column] = start

    def one_field(f, carry):
        for z in range(planes):
            span = slice(z * AREA, (z + 1) * AREA)
            picked[:, span] = jnp.dot(pick, sums_ref[f, :, span], preferred_element_type=jnp.float32)

        def one_column(column, carry):
            rows = pl.ds(pl.multiple_of(column * across, across), across)
            peaks = [jnp.zeros((across, LANES), jnp.float32)] * planes
            for c in range(AREA // LANES):
                values = [
                    picked[rows, z * AREA + c * LANES : z * AREA + (c + 1) * LANES]
                    for z in range(planes)
                ]
                for k, result in enumerate(filter_list(values, 0, planes)):
                    smoothed[k, :, c * LANES : (c + 1) * LANES] = result
                    peaks[k] = jnp.maximum(peaks[k], jnp.abs(result))
            for k in range(planes):
                peak = jnp.max(peaks[k], axis=1, keepdims=True)
                power = jnp.floor(jnp.log2(jnp.maximum(peak, 1e-30))) + 1.0
                scale = jnp.exp2(15.0 - power)
                code = jnp.clip(jnp.round(smoothed[k] * scale), -32767.0, 32767.0)
                code = jnp.concatenate([code[:, p * width : (p + 1) * width] for p in range(parts)], axis=0)
                where = k * down + column
                send_ref[where, :, pl.ds(pl.multiple_of(f * width, width), width)] = code.astype(
                    jnp.int32
                ).astype(jnp.int16)
                head[where] = jnp.where(lane == f, power.astype(jnp.int32), head[where])
            return carry

        return lax.fori_loop(0, down, one_column, carry)

    lax.fori_loop(0, fields, one_field, 0)
    full = fields * width
    for d in range(peers):
        block = head[d]
        if parts > 1:
            block = jnp.concatenate([block] * parts, axis=0)
        send_ref[d, :, full : full + LANES] = block.astype(jnp.int16)


def along_x(value, lane, row):
    count = value.shape[0]
    after = jnp.where(row == count - 1, 0.0, pltpu.roll(value, count - 1, 0))
    before = jnp.where(row == 0, 0.0, pltpu.roll(value, 1, 0))
    total = value * TAPS[0]
    for k in range(1, RADIUS + 1):
        right = pltpu.roll(jnp.where(lane < k, after, value), LANES - k, 1)
        left = pltpu.roll(jnp.where(lane >= LANES - k, before, value), k, 1)
        total = total + TAPS[k] * (right + left)
    return total


def deposit_kernel(across, fields, code_ref, head_ref, out_ref, tiles):
    f = pl.program_id(0)
    sources = code_ref.shape[0]
    parts = ROWS // across
    width = AREA // parts
    records = sources * across
    head = head_ref[...].astype(jnp.int32)[:, :across].reshape(records, LANES)
    place = head[:, fields : fields + 1]
    lane = lax.broadcasted_iota(jnp.int32, (records, LANES), 1)
    power = jnp.sum(jnp.where(lane == f, head, 0), axis=1, keepdims=True).astype(jnp.float32)
    scale = jnp.exp2(power - 15.0)
    row = lax.broadcasted_iota(jnp.int32, (records, TILES * across), 0)
    column = lax.broadcasted_iota(jnp.int32, (records, TILES * across), 1)
    hit = place * across + row % across == column
    low_land = jnp.where(hit, scale, 0.0).astype(jnp.bfloat16)
    high_land = (low_land.astype(jnp.float32) * 256.0).astype(jnp.bfloat16)
    contract = (((0,), (0,)), ((), ()))
    for p in range(parts):
        code = code_ref[...].astype(jnp.int32).reshape(sources, parts, across, width)[:, p]
        code = code.reshape(records, width)
        high = (code + 128) >> 8
        low = code - high * 256
        tiles[:, p * width : (p + 1) * width] = lax.dot_general(
            high_land, high.astype(jnp.float32).astype(jnp.bfloat16), contract, preferred_element_type=jnp.float32
        ) + lax.dot_general(
            low_land, low.astype(jnp.float32).astype(jnp.bfloat16), contract, preferred_element_type=jnp.float32
        )
    lane = lax.broadcasted_iota(jnp.int32, (across, LANES), 1)
    side = lax.broadcasted_iota(jnp.int32, (across, LANES), 0)

    def one_row(ly, carry):
        for c in range(AREA // LANES):
            cells = [
                tiles[pl.ds(pl.multiple_of((ly * BX + lx) * across, across), across), c * LANES : (c + 1) * LANES]
                for lx in range(BX)
            ]
            for a in range(LANES // TE):
                joined = cells[0] if a == 0 else pltpu.roll(cells[0], LANES - a * TE, 1)
                for lx in range(1, BX):
                    turn = (lx - a) * TE % LANES
                    moved = pltpu.roll(cells[lx], turn, 1) if turn else cells[lx]
                    joined = jnp.where(lane < lx * TE, joined, moved)
                out_ref[0, ly * TE + c * (LANES // TE) + a] = along_x(joined, lane, side)
        return carry

    lax.fori_loop(0, BY, one_row, 0)


def finish_kernel(across, mid_ref, above_ref, below_ref, out_ref, turned):
    height = mid_ref.shape[1]
    step = 8
    for y in range(0, height, step):
        values = []
        for r in range(y - RADIUS, y + step + RADIUS):
            if r < 0:
                values.append(above_ref[0, r + RADIUS])
            elif r >= height:
                values.append(below_ref[0, r - height])
            else:
                values.append(mid_ref[0, r])
        for k, result in enumerate(filter_list(values, -RADIUS, step)):
            turned[(y + k) * across : (y + k + 1) * across, :] = result
        for g in range(across):
            out_ref[0, 0, y : y + step, g * LANES : (g + 1) * LANES] = turned[
                pl.ds(y * across + g, step, stride=across), :
            ]


def local(across, down, tile_sums, tile_dest, tile_place, tile_count):
    slots, fields, cells = tile_sums.shape
    planes = cells // AREA
    peers = across * down
    parts = ROWS // across
    width = AREA // parts
    height = BY * TE
    params = pltpu.CompilerParams(vmem_limit_bytes=VMEM_BYTES)
    vmem = pl.BlockSpec(memory_space=pltpu.VMEM)
    send = pl.pallas_call(
        functools.partial(encode_kernel, across, down, planes),
        out_shape=jax.ShapeDtypeStruct((peers, ROWS, fields * width + LANES), jnp.int16),
        in_specs=[vmem] * 4,
        out_specs=vmem,
        scratch_shapes=[
            pltpu.VMEM((peers, cells), jnp.float32),
            pltpu.VMEM((planes, across, AREA), jnp.float32),
            pltpu.VMEM((peers, across, LANES), jnp.int32),
        ],
        compiler_params=params,
    )(
        tile_sums.transpose(1, 0, 2),
        tile_dest.reshape(1, slots),
        tile_place.reshape(1, slots),
        tile_count.reshape(1, 1),
    )
    got = lax.all_to_all(send, ("gx", "gy"), split_axis=0, concat_axis=0, tiled=True)
    mid = pl.pallas_call(
        functools.partial(deposit_kernel, across, fields),
        grid=(fields,),
        out_shape=jax.ShapeDtypeStruct((fields, height, across, LANES), jnp.float32),
        in_specs=[
            pl.BlockSpec((peers, ROWS, width), lambda f: (0, 0, f)),
            pl.BlockSpec((peers, ROWS, LANES), lambda f: (0, 0, fields * width // LANES)),
        ],
        out_specs=pl.BlockSpec((1, height, across, LANES), lambda f: (f, 0, 0, 0)),
        scratch_shapes=[pltpu.VMEM((TILES * across, AREA), jnp.float32)],
        compiler_params=params,
    )(got, got)
    up = [(i, i + 1) for i in range(down - 1)]
    above = lax.ppermute(mid[:, height - RADIUS :], "gy", up)
    below = lax.ppermute(mid[:, :RADIUS], "gy", [(j, i) for i, j in up])
    edge = pl.BlockSpec((1, RADIUS, across, LANES), lambda f: (f, 0, 0, 0))
    return pl.pallas_call(
        functools.partial(finish_kernel, across),
        grid=(fields,),
        out_shape=jax.ShapeDtypeStruct((fields, 1, height, across * LANES), jnp.float32),
        in_specs=[pl.BlockSpec((1, height, across, LANES), lambda f: (f, 0, 0, 0)), edge, edge],
        out_specs=pl.BlockSpec((1, 1, height, across * LANES), lambda f: (f, 0, 0, 0)),
        scratch_shapes=[pltpu.VMEM((height * across, LANES), jnp.float32)],
        compiler_params=params,
    )(mid, above, below)


def solution(mesh):
    across, down = mesh.shape["gx"], mesh.shape["gy"]
    return jax.shard_map(
        functools.partial(local, across, down),
        mesh=mesh,
        in_specs=(P(("gx", "gy"), None, None), P(("gx", "gy")), P(("gx", "gy")), P(("gx", "gy"))),
        out_specs=P(None, "gx", "gy", None),
        check_vma=False,
    )
```

time: 279 us -> 136 us (0.49)
  local copies, waits for them, and re-layouts: 67.3 us -> 1.56 us
  waiting for transfers between devices: 65 us -> 1.46 us
  Pallas kernels: 0 us -> 56.3 us
  other arithmetic: 35.8 us -> 0 us
  matrix products: 23.8 us -> 0 us
  starting transfers between devices: 24.6 us -> 5.56 us
  blocking collectives: 60.4 us -> 69.9 us
    all_to_all x2 -> x0, waiting for transfers between devices: 59 us -> none  [the longest x1 59 us: local(): lax.all_to_all(outgoing, ('gx', 'gy'), split_axis=0, concat_axis=0, tiled...]
    pallas_call x0 -> x3, Pallas kernels: none -> 56.3 us  [the longest x1 41.4 us: local(): pl.pallas_call(functools.partial(deposit_kernel, across, fields), grid=(f...]
    add x4 -> x0, other arithmetic: 24.1 us -> none  [the longest x3 23.5 us: smooth_axis(): result + taps[offset] * lax.slice_in_dim(padded, offset, offset + length,...]
    dot_general x2 -> x0, matrix products: 23.8 us -> none  [the longest x1 21.4 us: local(): deposited = jnp.dot(landing, incoming, preferred_element_type=jnp.float32)]
    dot_general x1 -> x0, local copies, waits for them, and re-layouts: 15.4 us -> none  [local(): deposited = jnp.dot(landing, incoming, preferred_element_type=jnp.float32)]
    all_to_all x2 -> x0, starting transfers between devices: 12.9 us -> none  [the longest x1 7.1 us: local(): lax.all_to_all(out_place[:, None], ('gx', 'gy'), split_axis=0, concat_axi...]
    transpose x1 -> x0, local copies, waits for them, and re-layouts: 12.1 us -> none  [local(): deposited.reshape(BY, BX, fields, planes, TE, TE)]
    unnamed x8 -> x4, local copies, waits for them, and re-layouts: 10.4 us -> 0.62 us
  transfers between devices with their start and end apart: 6 -> 2, of which waited for: 4 -> 2; matrix products, arithmetic and copies ran while one was open for 6% -> 0% of each run, Pallas kernels for 0% -> 0%
where the time goes in v1:
time: 136 us; the launch traced here: 135 us
  blocking collectives  69.9 us (51%)
  Pallas kernels  56.3 us (41%)
  starting transfers between devices  5.56 us (4%)
  local copies, waits for them, and re-layouts  1.56 us (1%)
  waiting for transfers between devices  1.46 us (1%)
    all_to_all x1, blocking collectives, local(): lax.all_to_all(send, ('gx', 'gy'), split_axis=0, concat_axis=0, tiled=True)  69.9 us
    pallas_call x1, Pallas kernels, local(): pl.pallas_call(functools.partial(deposit_kernel, across, fields), grid=(f...  41.4 us
    pallas_call x1, Pallas kernels, local(): pl.pallas_call(functools.partial(encode_kernel, across, down, planes), ou...  9.56 us
    pallas_call x1, Pallas kernels, local(): pl.pallas_call(functools.partial(finish_kernel, across), grid=(fields,),...  5.4 us
    ppermute x1, starting transfers between devices, local(): above = lax.ppermute(mid[:, height - RADIUS:], 'gy', up)  3.22 us
  transfers between devices with their start and end apart: 2, of which 2 were waited for; matrix products, arithmetic and copies ran while one was open for 0% of the time, Pallas kernels for 0%

profile of v1, /device:TPU:1, one launch (start us, length us, event | category | flops | bytes accessed | tf_op | source)
XLA Modules:
  0.0 135.5 jit_solution(18329054060607535211)
XLA Ops:
  0.7 9.6 %shard_map.46 = s16[32,16,2688]{2,1,0:T(8,128)(2,1)} custom-call(bf16[5,32,8192]{2,1,0:T(8,128)(2,1)} %bitcast.5, s32[1,32]{1,0:T(1,128)} %bitcast.6, s32[1,32]{1,0:T(1,128)} %bitcast.7, s32[1,1]{1,0:T(1,128)} %bitcast.4.count_ref), custom_call_target="tpu_custom_call" | custom-call | tf_op jit(solution)/shard_map/pallas_call | solution.py:198
  10.2 69.9 %all_to_all.5.code_ref.head_ref = s16[32,16,2688]{2,1,0:T(8,128)(2,1)} all-to-all(s16[32,16,2688]{2,1,0:T(8,128)(2,1)} %shard_map.46), channel_id=1, replica_groups=mesh['gx'=8,'gy'=4] {'gx','gy'}, dimensions={0} | all-to-all | bytes 5505024 | tf_op jit(solution)/shard_map/all_to_all | solution.py:215
  80.1 41.4 %shard_map.47.mid_ref = f32[5,128,8,128]{3,2,1,0:T(8,128)} custom-call(s16[32,16,2688]{2,1,0:T(8,128)(2,1)} %all_to_all.5.code_ref.head_ref, s16[32,16,2688]{2,1,0:T(8,128)(2,1)} %all_to_all.5.code_ref.head_ref), custom_call_target="tpu_custom_call" | custom-call | tf_op jit(solution)/shard_map/pallas_call | solution.py:216
  121.5 0.9 fusion
  122.4 2.3 %collective-permute-start.1 = (f32[5,4,8,128]{3,2,1,0:T(8,128)S(1)}, f32[5,4,8,128]{3,2,1,0:T(8,128)S(1)}, u32[]{:S(2)}, u32[]{:S(2)}) collective-permute-start(f32[5,4,8,128]{3,2,1,0:T(8,128)S(1)} %get-tuple-element.5), channel_id=1, source_target_pairs={{1,0},{2,1},{3,2},{5,4},{6,5},{7,6},{9,8},{10,9},{11,10},{13,12},{... | collective-permute-start | bytes 245768 | tf_op jit(solution)/shard_map/ppermute | solution.py:230
  124.8 3.2 %collective-permute-start = (f32[5,4,8,128]{3,2,1,0:T(8,128)S(1)}, f32[5,4,8,128]{3,2,1,0:T(8,128)S(1)}, u32[]{:S(2)}, u32[]{:S(2)}) collective-permute-start(f32[5,4,8,128]{3,2,1,0:T(8,128)S(1)} %get-tuple-element.6), channel_id=1, source_target_pairs={{0,1},{1,2},{2,3},{4,5},{5,6},{6,7},{8,9},{9,10},{10,11},{12,13},{... | collective-permute-start | bytes 245768 | tf_op jit(solution)/shard_map/ppermute | solution.py:229
  128.0 0.2 collective-permute-done.1.below_ref
  128.2 0.0 copy-start
  128.2 1.3 collective-permute-done.above_ref
  129.4 0.0 copy-done
  129.4 0.0 copy-start.1
  129.4 0.6 copy-done.1
  130.1 5.4 %shard_map.48 = f32[5,1,128,1024]{3,2,1,0:T(8,128)} custom-call(f32[5,128,8,128]{3,2,1,0:T(8,128)} %shard_map.47.mid_ref, f32[5,4,8,128]{3,2,1,0:T(8,128)} %copy-done.1, f32[5,4,8,128]{3,2,1,0:T(8,128)} %copy-done), custom_call_target="tpu_custom_call" | custom-call | tf_op jit(solution)/shard_map/pallas_call | solution.py:232
Async XLA Ops:
  122.4 5.8 %collective-permute-start.1 = (f32[5,4,8,128]{3,2,1,0:T(8,128)S(1)}, f32[5,4,8,128]{3,2,1,0:T(8,128)S(1)}, u32[]{:S(2)}, u32[]{:S(2)}) collective-permute-start(f32[5,4,8,128]{3,2,1,0:T(8,128)S(1)} %get-tuple-element.5), channel_id=1, source_target_pairs={{1,0},{2,1},{3,2},{5,4},{6,5},{7,6},{9,8},{10,9},{11,10},{13,12},{... | collective-permute-start | bytes 245768 | tf_op jit(solution)/shard_map/ppermute | solution.py:230
  124.8 4.7 %collective-permute-start = (f32[5,4,8,128]{3,2,1,0:T(8,128)S(1)}, f32[5,4,8,128]{3,2,1,0:T(8,128)S(1)}, u32[]{:S(2)}, u32[]{:S(2)}) collective-permute-start(f32[5,4,8,128]{3,2,1,0:T(8,128)S(1)} %get-tuple-element.6), channel_id=1, source_target_pairs={{0,1},{1,2},{2,3},{4,5},{5,6},{6,7},{8,9},{9,10},{10,11},{12,13},{... | collective-permute-start | bytes 245768 | tf_op jit(solution)/shard_map/ppermute | solution.py:229
  128.2 1.3 copy-start
  129.4 0.6 copy-start.1

commit v2 on v1

--- a/solution.py
+++ b/solution.py
@@ -3,6 +3,8 @@
 
 import jax
 import jax.numpy as jnp
+import ml_dtypes
+import numpy as np
 from jax import lax
 from jax.experimental import pallas as pl
 from jax.experimental.pallas import tpu as pltpu
@@ -106,20 +108,30 @@
         send_ref[d, :, full : full + LANES] = block.astype(jnp.int16)
 
 
-def along_x(value, lane, row):
-    count = value.shape[0]
-    after = jnp.where(row == count - 1, 0.0, pltpu.roll(value, count - 1, 0))
-    before = jnp.where(row == 0, 0.0, pltpu.roll(value, 1, 0))
-    total = value * TAPS[0]
-    for k in range(1, RADIUS + 1):
-        right = pltpu.roll(jnp.where(lane < k, after, value), LANES - k, 1)
-        left = pltpu.roll(jnp.where(lane >= LANES - k, before, value), k, 1)
-        total = total + TAPS[k] * (right + left)
-    return total
-
-
-def deposit_kernel(across, fields, code_ref, head_ref, out_ref, tiles):
-    f = pl.program_id(0)
+def turn_matrix():
+    band = np.zeros((BX * TE + 2 * TE, BX * TE))
+    taps = gauss_taps()
+    for x in range(BX * TE):
+        for k in range(-RADIUS, RADIUS + 1):
+            source = x + k
+            if source < 0:
+                source += BX * TE + 2 * TE
+            band[source, x] = taps[k + RADIUS]
+    per = LANES // TE
+    matrix = np.zeros((BX + 1, per, TE, per, BX * TE))
+    for a in range(per):
+        for lx in range(BX):
+            matrix[lx, a, :, a, :] = band[lx * TE : (lx + 1) * TE]
+        half = TE // 2
+        matrix[BX, a, :half, a, :] = band[BX * TE : BX * TE + half]
+        matrix[BX, a, half:, a, :] = band[BX * TE + 2 * TE - half :]
+    matrix = matrix.reshape((BX + 1) * LANES, per * BX * TE).astype(np.float32)
+    high = matrix.astype(ml_dtypes.bfloat16)
+    low = (matrix - high.astype(np.float32)).astype(ml_dtypes.bfloat16)
+    return high, low
+
+
+def land_tiles(across, fields, f, code_ref, head_ref, tiles):
     sources = code_ref.shape[0]
     parts = ROWS // across
     width = AREA // parts
@@ -132,35 +144,50 @@
     row = lax.broadcasted_iota(jnp.int32, (records, TILES * across), 0)
     column = lax.broadcasted_iota(jnp.int32, (records, TILES * across), 1)
     hit = place * across + row % across == column
-    low_land = jnp.where(hit, scale, 0.0).astype(jnp.bfloat16)
+    low_land = jnp.where(hit, scale, 0.0).T.astype(jnp.bfloat16)
     high_land = (low_land.astype(jnp.float32) * 256.0).astype(jnp.bfloat16)
-    contract = (((0,), (0,)), ((), ()))
     for p in range(parts):
         code = code_ref[...].astype(jnp.int32).reshape(sources, parts, across, width)[:, p]
         code = code.reshape(records, width)
         high = (code + 128) >> 8
         low = code - high * 256
-        tiles[:, p * width : (p + 1) * width] = lax.dot_general(
-            high_land, high.astype(jnp.float32).astype(jnp.bfloat16), contract, preferred_element_type=jnp.float32
-        ) + lax.dot_general(
-            low_land, low.astype(jnp.float32).astype(jnp.bfloat16), contract, preferred_element_type=jnp.float32
-        )
+        tiles[:, p * width : (p + 1) * width] = jnp.dot(
+            high_land, high.astype(jnp.float32).astype(jnp.bfloat16), preferred_element_type=jnp.float32
+        ) + jnp.dot(low_land, low.astype(jnp.float32).astype(jnp.bfloat16), preferred_element_type=jnp.float32)
+
+
+def turn_row(across, ly, tiles, turn_high_ref, turn_low_ref):
     lane = lax.broadcasted_iota(jnp.int32, (across, LANES), 1)
     side = lax.broadcasted_iota(jnp.int32, (across, LANES), 0)
+    lines = []
+    for c in range(AREA // LANES):
+        cells = [
+            tiles[pl.ds(pl.multiple_of((ly * BX + lx) * across, across), across), c * LANES : (c + 1) * LANES]
+            for lx in range(BX)
+        ]
+        after = jnp.where(side == across - 1, 0.0, pltpu.roll(cells[0], across - 1, 0))
+        before = jnp.where(side == 0, 0.0, pltpu.roll(cells[BX - 1], 1, 0))
+        cells.append(jnp.where(lane % TE < TE // 2, after, before))
+        lines.append(jnp.concatenate(cells, axis=1))
+    whole = jnp.concatenate(lines, axis=0)
+    high = whole.astype(jnp.bfloat16)
+    low = (whole - high.astype(jnp.float32)).astype(jnp.bfloat16)
+    return (
+        jnp.dot(high, turn_high_ref[...], preferred_element_type=jnp.float32)
+        + jnp.dot(low, turn_high_ref[...], preferred_element_type=jnp.float32)
+        + jnp.dot(high, turn_low_ref[...], preferred_element_type=jnp.float32)
+    )
+
+
+def deposit_kernel(across, fields, code_ref, head_ref, turn_high_ref, turn_low_ref, out_ref, tiles):
+    land_tiles(across, fields, pl.program_id(0), code_ref, head_ref, tiles)
+    per = LANES // TE
 
     def one_row(ly, carry):
+        turned = turn_row(across, ly, tiles, turn_high_ref, turn_low_ref)
         for c in range(AREA // LANES):
-            cells = [
-                tiles[pl.ds(pl.multiple_of((ly * BX + lx) * across, across), across), c * LANES : (c + 1) * LANES]
-                for lx in range(BX)
-            ]
-            for a in range(LANES // TE):
-                joined = cells[0] if a == 0 else pltpu.roll(cells[0], LANES - a * TE, 1)
-                for lx in range(1, BX):
-                    turn = (lx - a) * TE % LANES
-                    moved = pltpu.roll(cells[lx], turn, 1) if turn else cells[lx]
-                    joined = jnp.where(lane < lx * TE, joined, moved)
-                out_ref[0, ly * TE + c * (LANES // TE) + a] = along_x(joined, lane, side)
+            for a in range(per):
+                out_ref[0, ly * TE + c * per + a] = turned[c * across : (c + 1) * across, a * LANES : (a + 1) * LANES]
         return carry
 
     lax.fori_loop(0, BY, one_row, 0)
@@ -220,11 +247,13 @@
         in_specs=[
             pl.BlockSpec((peers, ROWS, width), lambda f: (0, 0, f)),
             pl.BlockSpec((peers, ROWS, LANES), lambda f: (0, 0, fields * width // LANES)),
+            vmem,
+            vmem,
         ],
         out_specs=pl.BlockSpec((1, height, across, LANES), lambda f: (f, 0, 0, 0)),
         scratch_shapes=[pltpu.VMEM((TILES * across, AREA), jnp.float32)],
         compiler_params=params,
-    )(got, got)
+    )(got, got, *turn_matrix())
     up = [(i, i + 1) for i in range(down - 1)]
     above = lax.ppermute(mid[:, height - RADIUS :], "gy", up)
     below = lax.ppermute(mid[:, :RADIUS], "gy", [(j, i) for i, j in up])

time: 136 us -> 110 us (0.81)
  Pallas kernels: 56.3 us -> 30 us
    pallas_call x1, Pallas kernels: 41.4 us -> 15 us  [local(): pl.pallas_call(functools.partial(deposit_kernel, across, fields), grid=(f...]
where the time goes in v2:
time: 110 us; the launch traced here: 109 us
  blocking collectives  69.9 us (64%)
  Pallas kernels  30 us (27%)
  starting transfers between devices  5.56 us (5%)
  local copies, waits for them, and re-layouts  1.56 us (1%)
  waiting for transfers between devices  1.46 us (1%)
    all_to_all x1, blocking collectives, local(): lax.all_to_all(send, ('gx', 'gy'), split_axis=0, concat_axis=0, tiled=True)  69.9 us
    pallas_call x1, Pallas kernels, local(): pl.pallas_call(functools.partial(deposit_kernel, across, fields), grid=(f...  15 us
    pallas_call x1, Pallas kernels, local(): pl.pallas_call(functools.partial(encode_kernel, across, down, planes), ou...  9.56 us
    pallas_call x1, Pallas kernels, local(): pl.pallas_call(functools.partial(finish_kernel, across), grid=(fields,),...  5.4 us
    ppermute x1, starting transfers between devices, local(): above = lax.ppermute(mid[:, height - RADIUS:], 'gy', up)  3.22 us
    ppermute x1, starting transfers between devices, local(): below = lax.ppermute(mid[:, :RADIUS], 'gy', [(j, i) for i, j in up])  2.35 us
  transfers between devices with their start and end apart: 2, of which 2 were waited for; matrix products, arithmetic and copies ran while one was open for 0% of the time, Pallas kernels for 0%

profile of v2, /device:TPU:1, one launch (start us, length us, event | category | flops | bytes accessed | tf_op | source)
XLA Modules:
  0.0 109.1 jit_solution(14298363441334069177)
XLA Ops:
  0.7 9.6 %shard_map.64 = s16[32,16,2688]{2,1,0:T(8,128)(2,1)} custom-call(bf16[5,32,8192]{2,1,0:T(8,128)(2,1)} %bitcast.5, s32[1,32]{1,0:T(1,128)} %bitcast.6, s32[1,32]{1,0:T(1,128)} %bitcast.7, s32[1,1]{1,0:T(1,128)} %bitcast.4.count_ref), custom_call_target="tpu_custom_call" | custom-call | tf_op jit(solution)/shard_map/pallas_call | solution.py:225
  10.2 69.9 %all_to_all.5.code_ref.head_ref = s16[32,16,2688]{2,1,0:T(8,128)(2,1)} all-to-all(s16[32,16,2688]{2,1,0:T(8,128)(2,1)} %shard_map.64), channel_id=1, replica_groups=mesh['gx'=8,'gy'=4] {'gx','gy'}, dimensions={0} | all-to-all | bytes 5505024 | tf_op jit(solution)/shard_map/all_to_all | solution.py:242
  80.1 15.0 %shard_map.65.mid_ref = f32[5,128,8,128]{3,2,1,0:T(8,128)} custom-call(s16[32,16,2688]{2,1,0:T(8,128)(2,1)} %all_to_all.5.code_ref.head_ref, s16[32,16,2688]{2,1,0:T(8,128)(2,1)} %all_to_all.5.code_ref.head_ref, bf16[640,512]{1,0:T(8,128)(2,1)} %constant.4.clone.turn_high_ref, bf16[640,512]{1,0:T(8,128)(2,1)} %constant.5.clone.turn_low_ref), custom_call_target="tpu_custom_call" | custom-call | tf_op jit(solution)/shard_map/pallas_call | solution.py:243
  95.1 0.9 fusion
  96.1 2.3 %collective-permute-start.1 = (f32[5,4,8,128]{3,2,1,0:T(8,128)S(1)}, f32[5,4,8,128]{3,2,1,0:T(8,128)S(1)}, u32[]{:S(2)}, u32[]{:S(2)}) collective-permute-start(f32[5,4,8,128]{3,2,1,0:T(8,128)S(1)} %get-tuple-element.5), channel_id=1, source_target_pairs={{1,0},{2,1},{3,2},{5,4},{6,5},{7,6},{9,8},{10,9},{11,10},{13,12},{... | collective-permute-start | bytes 245768 | tf_op jit(solution)/shard_map/ppermute | solution.py:259
  98.4 3.2 %collective-permute-start = (f32[5,4,8,128]{3,2,1,0:T(8,128)S(1)}, f32[5,4,8,128]{3,2,1,0:T(8,128)S(1)}, u32[]{:S(2)}, u32[]{:S(2)}) collective-permute-start(f32[5,4,8,128]{3,2,1,0:T(8,128)S(1)} %get-tuple-element.6), channel_id=1, source_target_pairs={{0,1},{1,2},{2,3},{4,5},{5,6},{6,7},{8,9},{9,10},{10,11},{12,13},{... | collective-permute-start | bytes 245768 | tf_op jit(solution)/shard_map/ppermute | solution.py:258
  101.6 0.2 collective-permute-done.1.below_ref
  101.8 0.0 copy-start
  101.8 1.3 %collective-permute-done.above_ref = f32[5,4,8,128]{3,2,1,0:T(8,128)S(1)} collective-permute-done((f32[5,4,8,128]{3,2,1,0:T(8,128)S(1)}, f32[5,4,8,128]{3,2,1,0:T(8,128)S(1)}, u32[]{:S(2)}, u32[]{:S(2)}) %collective-permute-start) | collective-permute-done | bytes 81952 | tf_op jit(solution)/shard_map/ppermute | solution.py:258
  103.1 0.0 copy-done
  103.1 0.0 copy-start.1
  103.1 0.6 copy-done.1
  103.7 5.4 %shard_map.66 = f32[5,1,128,1024]{3,2,1,0:T(8,128)} custom-call(f32[5,128,8,128]{3,2,1,0:T(8,128)} %shard_map.65.mid_ref, f32[5,4,8,128]{3,2,1,0:T(8,128)} %copy-done.1, f32[5,4,8,128]{3,2,1,0:T(8,128)} %copy-done), custom_call_target="tpu_custom_call" | custom-call | tf_op jit(solution)/shard_map/pallas_call | solution.py:261
Async XLA Ops:
  96.1 5.8 %collective-permute-start.1 = (f32[5,4,8,128]{3,2,1,0:T(8,128)S(1)}, f32[5,4,8,128]{3,2,1,0:T(8,128)S(1)}, u32[]{:S(2)}, u32[]{:S(2)}) collective-permute-start(f32[5,4,8,128]{3,2,1,0:T(8,128)S(1)} %get-tuple-element.5), channel_id=1, source_target_pairs={{1,0},{2,1},{3,2},{5,4},{6,5},{7,6},{9,8},{10,9},{11,10},{13,12},{... | collective-permute-start | bytes 245768 | tf_op jit(solution)/shard_map/ppermute | solution.py:259
  98.4 4.7 %collective-permute-start = (f32[5,4,8,128]{3,2,1,0:T(8,128)S(1)}, f32[5,4,8,128]{3,2,1,0:T(8,128)S(1)}, u32[]{:S(2)}, u32[]{:S(2)}) collective-permute-start(f32[5,4,8,128]{3,2,1,0:T(8,128)S(1)} %get-tuple-element.6), channel_id=1, source_target_pairs={{0,1},{1,2},{2,3},{4,5},{5,6},{6,7},{8,9},{9,10},{10,11},{12,13},{... | collective-permute-start | bytes 245768 | tf_op jit(solution)/shard_map/ppermute | solution.py:258
  101.8 1.3 %copy-start = (f32[5,4,8,128]{3,2,1,0:T(8,128)}, f32[5,4,8,128]{3,2,1,0:T(8,128)S(1)}, u32[]{:S(2)}) copy-start(f32[5,4,8,128]{3,2,1,0:T(8,128)S(1)} %collective-permute-done.1.below_ref) | copy-start | bytes 245764
  103.1 0.6 copy-start.1

commit v3 on v2

--- a/solution.py
+++ b/solution.py
@@ -51,61 +51,74 @@
     return results
 
 
-def encode_kernel(across, down, planes, sums_ref, dest_ref, place_ref, count_ref, send_ref, picked, smoothed, head):
-    fields, slots, cells = sums_ref.shape
-    parts = ROWS // across
-    width = AREA // parts
-    peers = across * down
+def encode_start(across, down, planes, fields, dest_ref, place_ref, count_ref, head):
+    peers, slots = across * down, dest_ref.shape[1]
     row = lax.broadcasted_iota(jnp.int32, (peers, slots), 0)
     slot = lax.broadcasted_iota(jnp.int32, (peers, slots), 1)
     target = (row % across) * down + row // across
     chosen = (dest_ref[...] == target) & (slot < count_ref[...])
-    pick = jnp.where(chosen, 1.0, 0.0).astype(jnp.bfloat16)
     place = jnp.sum(jnp.where(chosen, place_ref[...] + 1, 0), axis=1, keepdims=True) - 1
     lane = lax.broadcasted_iota(jnp.int32, (across, LANES), 1)
     for column in range(down):
         start = jnp.where(lane == fields, place[column * across : (column + 1) * across], 0)
         for k in range(planes):
             head[k * down + column] = start
+    return jnp.where(chosen, 1.0, 0.0).astype(jnp.bfloat16)
+
+
+def encode_field(across, down, planes, f, pick, sums_ref, picked, smoothed, head, put):
+    parts = ROWS // across
+    width = AREA // parts
+    lane = lax.broadcasted_iota(jnp.int32, (across, LANES), 1)
+    for z in range(planes):
+        span = slice(z * AREA, (z + 1) * AREA)
+        picked[:, span] = jnp.dot(pick, sums_ref[f, :, span], preferred_element_type=jnp.float32)
+
+    def one_column(column, carry):
+        rows = pl.ds(pl.multiple_of(column * across, across), across)
+        peaks = [jnp.zeros((across, LANES), jnp.float32)] * planes
+        for c in range(AREA // LANES):
+            values = [
+                picked[rows, z * AREA + c * LANES : z * AREA + (c + 1) * LANES]
+                for z in range(planes)
+            ]
+            for k, result in enumerate(filter_list(values, 0, planes)):
+                smoothed[k, :, c * LANES : (c + 1) * LANES] = result
+                peaks[k] = jnp.maximum(peaks[k], jnp.abs(result))
+        for k in range(planes):
+            peak = jnp.max(peaks[k], axis=1, keepdims=True)
+            power = jnp.floor(jnp.log2(jnp.maximum(peak, 1e-30))) + 1.0
+            scale = jnp.exp2(15.0 - power)
+            code = jnp.clip(jnp.round(smoothed[k] * scale), -32767.0, 32767.0)
+            code = jnp.concatenate([code[:, p * width : (p + 1) * width] for p in range(parts)], axis=0)
+            where = k * down + column
+            put(f, where, code.astype(jnp.int32).astype(jnp.int16))
+            head[where] = jnp.where(lane == f, power.astype(jnp.int32), head[where])
+        return carry
+
+    lax.fori_loop(0, down, one_column, 0)
+
+
+def full_head(across, block):
+    return jnp.concatenate([block] * (ROWS // across), axis=0).astype(jnp.int16)
+
+
+def encode_kernel(across, down, planes, sums_ref, dest_ref, place_ref, count_ref, send_ref, picked, smoothed, head):
+    fields = sums_ref.shape[0]
+    width = AREA * across // ROWS
+    pick = encode_start(across, down, planes, fields, dest_ref, place_ref, count_ref, head)
+
+    def put(f, where, code):
+        send_ref[where, :, pl.ds(pl.multiple_of(f * width, width), width)] = code
 
     def one_field(f, carry):
-        for z in range(planes):
-            span = slice(z * AREA, (z + 1) * AREA)
-            picked[:, span] = jnp.dot(pick, sums_ref[f, :, span], preferred_element_type=jnp.float32)
-
-        def one_column(column, carry):
-            rows = pl.ds(pl.multiple_of(column * across, across), across)
-            peaks = [jnp.zeros((across, LANES), jnp.float32)] * planes
-            for c in range(AREA // LANES):
-                values = [
-                    picked[rows, z * AREA + c * LANES : z * AREA + (c + 1) * LANES]
-                    for z in range(planes)
-                ]
-                for k, result in enumerate(filter_list(values, 0, planes)):
-                    smoothed[k, :, c * LANES : (c + 1) * LANES] = result
-                    peaks[k] = jnp.maximum(peaks[k], jnp.abs(result))
-            for k in range(planes):
-                peak = jnp.max(peaks[k], axis=1, keepdims=True)
-                power = jnp.floor(jnp.log2(jnp.maximum(peak, 1e-30))) + 1.0
-                scale = jnp.exp2(15.0 - power)
-                code = jnp.clip(jnp.round(smoothed[k] * scale), -32767.0, 32767.0)
-                code = jnp.concatenate([code[:, p * width : (p + 1) * width] for p in range(parts)], axis=0)
-                where = k * down + column
-                send_ref[where, :, pl.ds(pl.multiple_of(f * width, width), width)] = code.astype(
-                    jnp.int32
-                ).astype(jnp.int16)
-                head[where] = jnp.where(lane == f, power.astype(jnp.int32), head[where])
-            return carry
-
-        return lax.fori_loop(0, down, one_column, carry)
+        encode_field(across, down, planes, f, pick, sums_ref, picked, smoothed, head, put)
+        return carry
 
     lax.fori_loop(0, fields, one_field, 0)
     full = fields * width
-    for d in range(peers):
-        block = head[d]
-        if parts > 1:
-            block = jnp.concatenate([block] * parts, axis=0)
-        send_ref[d, :, full : full + LANES] = block.astype(jnp.int16)
+    for d in range(across * down):
+        send_ref[d, :, full : full + LANES] = full_head(across, head[d])
 
 
 def turn_matrix():
@@ -193,6 +206,152 @@
     lax.fori_loop(0, BY, one_row, 0)
 
 
+def exchange_kernel(
+    across, down, planes, sums_ref, dest_ref, place_ref, count_ref, turn_high_ref, turn_low_ref,
+    mid_ref, above_ref, below_ref, picked, smoothed, head, send, send_head, got, got_head, tiles, halo,
+    send_sem, recv_sem, own_sem, halo_send_sem, halo_recv_sem,
+):
+    fields = sums_ref.shape[0]
+    peers = across * down
+    height = mid_ref.shape[1]
+    my_x, my_y = lax.axis_index("gx"), lax.axis_index("gy")
+    me = my_x * down + my_y
+
+    barrier = pltpu.get_barrier_semaphore()
+
+    def greet(j, carry):
+        peer = (me + j) % peers
+        pl.semaphore_signal(
+            barrier, inc=1, device_id=(peer // down, peer % down), device_id_type=pl.DeviceIdType.MESH
+        )
+        return carry
+
+    lax.fori_loop(1, peers, greet, 0)
+
+    def post(source, target, sem):
+        def one(j, carry):
+            peer = (me + j) % peers
+            pltpu.make_async_remote_copy(
+                src_ref=source.at[peer],
+                dst_ref=target.at[me],
+                send_sem=send_sem.at[sem],
+                recv_sem=recv_sem.at[sem],
+                device_id=(peer // down, peer % down),
+                device_id_type=pl.DeviceIdType.MESH,
+            ).start()
+            return carry
+
+        lax.fori_loop(1, peers, one, 0)
+        pltpu.make_async_copy(source.at[me], target.at[me], own_sem.at[sem]).start()
+
+    def arrived(source, target, sem):
+        rest = pl.ds(0, peers - 1)
+        pltpu.make_async_copy(source.at[rest], target.at[rest], send_sem.at[sem]).wait()
+        pltpu.make_async_copy(source.at[rest], target.at[rest], recv_sem.at[sem]).wait()
+        pltpu.make_async_copy(source.at[me], target.at[me], own_sem.at[sem]).wait()
+
+    pick = encode_start(across, down, planes, fields, dest_ref, place_ref, count_ref, head)
+
+    def put(f, where, code):
+        send[f, where] = code
+
+    def encode(f, carry):
+        encode_field(across, down, planes, f, pick, sums_ref, picked, smoothed, head, put)
+        return carry
+
+    encode(0, 0)
+    pl.semaphore_wait(barrier, peers - 1)
+    post(send.at[0], got.at[0], 0)
+    lax.fori_loop(1, fields, encode, 0)
+    for d in range(peers):
+        send_head[d] = full_head(across, head[d])
+    post(send_head, got_head, fields)
+
+    def post_field(f, carry):
+        post(send.at[f], got.at[f], f)
+        return carry
+
+    lax.fori_loop(1, fields, post_field, 0)
+
+    def to_before(f):
+        return pltpu.make_async_remote_copy(
+            src_ref=mid_ref.at[f, pl.ds(0, RADIUS)],
+            dst_ref=halo.at[1, f],
+            send_sem=halo_send_sem.at[1, f],
+            recv_sem=halo_recv_sem.at[1, f],
+            device_id=(my_x, my_y - 1),
+            device_id_type=pl.DeviceIdType.MESH,
+        )
+
+    def to_after(f):
+        return pltpu.make_async_remote_copy(
+            src_ref=mid_ref.at[f, pl.ds(height - RADIUS, RADIUS)],
+            dst_ref=halo.at[0, f],
+            send_sem=halo_send_sem.at[0, f],
+            recv_sem=halo_recv_sem.at[0, f],
+            device_id=(my_x, my_y + 1),
+            device_id_type=pl.DeviceIdType.MESH,
+        )
+
+    arrived(send_head, got_head, fields)
+    per = LANES // TE
+
+    def deposit(f, carry):
+        arrived(send.at[f], got.at[f], f)
+        land_tiles(across, fields, f, got.at[f], got_head, tiles)
+
+        def one_row(ly, inner):
+            turned = turn_row(across, ly, tiles, turn_high_ref, turn_low_ref)
+            for c in range(AREA // LANES):
+                for a in range(per):
+                    mid_ref[f, ly * TE + c * per + a] = turned[
+                        c * across : (c + 1) * across, a * LANES : (a + 1) * LANES
+                    ]
+            return inner
+
+        lax.fori_loop(0, BY, one_row, 0)
+
+        @pl.when(my_y > 0)
+        def _():
+            to_before(f).start()
+
+        @pl.when(my_y < down - 1)
+        def _():
+            to_after(f).start()
+
+        return carry
+
+    lax.fori_loop(0, fields, deposit, 0)
+
+    @pl.when(my_y > 0)
+    def _():
+        def one(f, carry):
+            to_before(f).wait_send()
+            to_after(f).wait_recv()
+            return carry
+
+        lax.fori_loop(0, fields, one, 0)
+        above_ref[...] = halo[0]
+
+    @pl.when(my_y == 0)
+    def _():
+        above_ref[...] = jnp.zeros_like(above_ref)
+
+    @pl.when(my_y < down - 1)
+    def _():
+        def one(f, carry):
+            to_after(f).wait_send()
+            to_before(f).wait_recv()
+            return carry
+
+        lax.fori_loop(0, fields, one, 0)
+        below_ref[...] = halo[1]
+
+    @pl.when(my_y == down - 1)
+    def _():
+        below_ref[...] = jnp.zeros_like(below_ref)
+
+
 def finish_kernel(across, mid_ref, above_ref, below_ref, out_ref, turned):
     height = mid_ref.shape[1]
     step = 8
@@ -213,12 +372,45 @@
             ]
 
 
-def local(across, down, tile_sums, tile_dest, tile_place, tile_count):
-    slots, fields, cells = tile_sums.shape
-    planes = cells // AREA
+def by_exchange(across, down, planes, fields, operands):
     peers = across * down
-    parts = ROWS // across
-    width = AREA // parts
+    width = AREA * across // ROWS
+    height = BY * TE
+    vmem = pl.BlockSpec(memory_space=pltpu.VMEM)
+    return pl.pallas_call(
+        functools.partial(exchange_kernel, across, down, planes),
+        out_shape=[
+            jax.ShapeDtypeStruct((fields, height, across, LANES), jnp.float32),
+            jax.ShapeDtypeStruct((fields, RADIUS, across, LANES), jnp.float32),
+            jax.ShapeDtypeStruct((fields, RADIUS, across, LANES), jnp.float32),
+        ],
+        in_specs=[vmem] * 6,
+        out_specs=[vmem] * 3,
+        scratch_shapes=[
+            pltpu.VMEM((peers, planes * AREA), jnp.float32),
+            pltpu.VMEM((planes, across, AREA), jnp.float32),
+            pltpu.VMEM((peers, across, LANES), jnp.int32),
+            pltpu.VMEM((fields, peers, ROWS, width), jnp.int16),
+            pltpu.VMEM((peers, ROWS, LANES), jnp.int16),
+            pltpu.VMEM((fields, peers, ROWS, width), jnp.int16),
+            pltpu.VMEM((peers, ROWS, LANES), jnp.int16),
+            pltpu.VMEM((TILES * across, AREA), jnp.float32),
+            pltpu.VMEM((2, fields, RADIUS, across, LANES), jnp.float32),
+            pltpu.SemaphoreType.DMA((fields + 1,)),
+            pltpu.SemaphoreType.DMA((fields + 1,)),
+            pltpu.SemaphoreType.DMA((fields + 1,)),
+            pltpu.SemaphoreType.DMA((2, fields)),
+            pltpu.SemaphoreType.DMA((2, fields)),
+        ],
+        compiler_params=pltpu.CompilerParams(
+            vmem_limit_bytes=VMEM_BYTES, collective_id=0, has_side_effects=True
+        ),
+    )(*operands, *turn_matrix())
+
+
+def by_all_to_all(across, down, planes, fields, operands):
+    peers = across * down
+    width = AREA * across // ROWS
     height = BY * TE
     params = pltpu.CompilerParams(vmem_limit_bytes=VMEM_BYTES)
     vmem = pl.BlockSpec(memory_space=pltpu.VMEM)
@@ -228,17 +420,12 @@
         in_specs=[vmem] * 4,
         out_specs=vmem,
         scratch_shapes=[
-            pltpu.VMEM((peers, cells), jnp.float32),
+            pltpu.VMEM((peers, planes * AREA), jnp.float32),
             pltpu.VMEM((planes, across, AREA), jnp.float32),
             pltpu.VMEM((peers, across, LANES), jnp.int32),
         ],
         compiler_params=params,
-    )(
-        tile_sums.transpose(1, 0, 2),
-        tile_dest.reshape(1, slots),
-        tile_place.reshape(1, slots),
-        tile_count.reshape(1, 1),
-    )
+    )(*operands)
     got = lax.all_to_all(send, ("gx", "gy"), split_axis=0, concat_axis=0, tiled=True)
     mid = pl.pallas_call(
         functools.partial(deposit_kernel, across, fields),
@@ -257,6 +444,22 @@
     up = [(i, i + 1) for i in range(down - 1)]
     above = lax.ppermute(mid[:, height - RADIUS :], "gy", up)
     below = lax.ppermute(mid[:, :RADIUS], "gy", [(j, i) for i, j in up])
+    return mid, above, below
+
+
+def local(across, down, tile_sums, tile_dest, tile_place, tile_count):
+    slots, fields, cells = tile_sums.shape
+    planes = cells // AREA
+    height = BY * TE
+    operands = (
+        tile_sums.transpose(1, 0, 2),
+        tile_dest.reshape(1, slots),
+        tile_place.reshape(1, slots),
+        tile_count.reshape(1, 1),
+    )
+    fits = 8 * fields * slots * cells < VMEM_BYTES
+    plan = by_exchange if fits else by_all_to_all
+    mid, above, below = plan(across, down, planes, fields, operands)
     edge = pl.BlockSpec((1, RADIUS, across, LANES), lambda f: (f, 0, 0, 0))
     return pl.pallas_call(
         functools.partial(finish_kernel, across),
@@ -265,7 +468,7 @@
         in_specs=[pl.BlockSpec((1, height, across, LANES), lambda f: (f, 0, 0, 0)), edge, edge],
         out_specs=pl.BlockSpec((1, 1, height, across * LANES), lambda f: (f, 0, 0, 0)),
         scratch_shapes=[pltpu.VMEM((height * across, LANES), jnp.float32)],
-        compiler_params=params,
+        compiler_params=pltpu.CompilerParams(vmem_limit_bytes=VMEM_BYTES),
     )(mid, above, below)
 
 

time: 110 us -> 80.9 us (0.74)
  the two profiles are of different devices: /device:TPU:1 before, /device:TPU:13 now
where the time goes in v3:
time: 80.9 us; the launch traced here: 80.7 us
  Pallas kernels  80 us (99%)
    pallas_call x1, Pallas kernels, by_exchange(): pl.pallas_call(functools.partial(exchange_kernel, across, down, planes),...  74.6 us
    pallas_call x1, Pallas kernels, local(): pl.pallas_call(functools.partial(finish_kernel, across), grid=(fields,),...  5.41 us

profile of v3, /device:TPU:13, one launch (start us, length us, event | category | flops | bytes accessed | tf_op | source)
XLA Modules:
  0.0 80.7 jit_solution(4875051716329057677)
XLA Ops:
  0.7 74.6 %shard_map.64 = (f32[5,128,8,128]{3,2,1,0:T(8,128)}, f32[5,4,8,128]{3,2,1,0:T(8,128)}, f32[5,4,8,128]{3,2,1,0:T(8,128)}) custom-call(bf16[5,32,8192]{2,1,0:T(8,128)(2,1)} %bitcast.5, s32[1,32]{1,0:T(1,128)} %bitcast.6, s32[1,32]{1,0:T(1,128)} %bitcast.7, s32[1,1]{1,0:T(1,128)} %bitcast.4.count_ref, bf16[640,512]{1,0:T(8,128)(2,1)} %constant.4.clone.turn_high_ref, ...), custom_call_target="tpu_custom_call" | custom-call | tf_op jit(solution)/shard_map/pallas_call | solution.py:380
  75.3 5.4 %shard_map.65 = f32[5,1,128,1024]{3,2,1,0:T(8,128)} custom-call(f32[5,128,8,128]{3,2,1,0:T(8,128)} %get-tuple-element.8.mid_ref, f32[5,4,8,128]{3,2,1,0:T(8,128)} %get-tuple-element.9.above_ref, f32[5,4,8,128]{3,2,1,0:T(8,128)} %get-tuple-element.10.below_ref), custom_call_target="tpu_custom_call" | custom-call | tf_op jit(solution)/shard_map/pallas_call | solution.py:464

commit v4 on v3

--- a/solution.py
+++ b/solution.py
@@ -51,6 +51,12 @@
     return results
 
 
+def head_spot(across):
+    lane = lax.broadcasted_iota(jnp.int32, (across, LANES), 1)
+    row = lax.broadcasted_iota(jnp.int32, (across, LANES), 0)
+    return jnp.where(lane // 8 == row, lane % 8, -1)
+
+
 def encode_start(across, down, planes, fields, dest_ref, place_ref, count_ref, head):
     peers, slots = across * down, dest_ref.shape[1]
     row = lax.broadcasted_iota(jnp.int32, (peers, slots), 0)
@@ -58,23 +64,24 @@
     target = (row % across) * down + row // across
     chosen = (dest_ref[...] == target) & (slot < count_ref[...])
     place = jnp.sum(jnp.where(chosen, place_ref[...] + 1, 0), axis=1, keepdims=True) - 1
-    lane = lax.broadcasted_iota(jnp.int32, (across, LANES), 1)
+    spot = head_spot(across)
     for column in range(down):
-        start = jnp.where(lane == fields, place[column * across : (column + 1) * across], 0)
+        start = jnp.where(spot == fields, place[column * across : (column + 1) * across], 0)
         for k in range(planes):
             head[k * down + column] = start
     return jnp.where(chosen, 1.0, 0.0).astype(jnp.bfloat16)
 
 
-def encode_field(across, down, planes, f, pick, sums_ref, picked, smoothed, head, put):
+def encode_field(across, down, planes, f, pick, sums_ref, picked, smoothed, head, put, first=0, after=None):
     parts = ROWS // across
     width = AREA // parts
-    lane = lax.broadcasted_iota(jnp.int32, (across, LANES), 1)
+    spot = head_spot(across)
     for z in range(planes):
         span = slice(z * AREA, (z + 1) * AREA)
         picked[:, span] = jnp.dot(pick, sums_ref[f, :, span], preferred_element_type=jnp.float32)
 
-    def one_column(column, carry):
+    def one_column(index, carry):
+        column = (index + first) % down
         rows = pl.ds(pl.multiple_of(column * across, across), across)
         peaks = [jnp.zeros((across, LANES), jnp.float32)] * planes
         for c in range(AREA // LANES):
@@ -93,7 +100,9 @@
             code = jnp.concatenate([code[:, p * width : (p + 1) * width] for p in range(parts)], axis=0)
             where = k * down + column
             put(f, where, code.astype(jnp.int32).astype(jnp.int16))
-            head[where] = jnp.where(lane == f, power.astype(jnp.int32), head[where])
+            head[where] = jnp.where(spot == f, power.astype(jnp.int32), head[where])
+        if after is not None:
+            after(column)
         return carry
 
     lax.fori_loop(0, down, one_column, 0)
@@ -144,15 +153,14 @@
     return high, low
 
 
-def land_tiles(across, fields, f, code_ref, head_ref, tiles):
+def land_tiles(across, fields, f, code_ref, head, tiles):
     sources = code_ref.shape[0]
     parts = ROWS // across
     width = AREA // parts
     records = sources * across
-    head = head_ref[...].astype(jnp.int32)[:, :across].reshape(records, LANES)
-    place = head[:, fields : fields + 1]
-    lane = lax.broadcasted_iota(jnp.int32, (records, LANES), 1)
-    power = jnp.sum(jnp.where(lane == f, head, 0), axis=1, keepdims=True).astype(jnp.float32)
+    spot = head_spot(across)[None]
+    place = jnp.sum(jnp.where(spot == fields, head, 0), axis=2, keepdims=True).reshape(records, 1)
+    power = jnp.sum(jnp.where(spot == f, head, 0), axis=2, keepdims=True).reshape(records, 1).astype(jnp.float32)
     scale = jnp.exp2(power - 15.0)
     row = lax.broadcasted_iota(jnp.int32, (records, TILES * across), 0)
     column = lax.broadcasted_iota(jnp.int32, (records, TILES * across), 1)
@@ -169,7 +177,7 @@
         ) + jnp.dot(low_land, low.astype(jnp.float32).astype(jnp.bfloat16), preferred_element_type=jnp.float32)
 
 
-def turn_row(across, ly, tiles, turn_high_ref, turn_low_ref):
+def tile_rows(across, ly, tiles):
     lane = lax.broadcasted_iota(jnp.int32, (across, LANES), 1)
     side = lax.broadcasted_iota(jnp.int32, (across, LANES), 0)
     lines = []
@@ -184,7 +192,10 @@
         lines.append(jnp.concatenate(cells, axis=1))
     whole = jnp.concatenate(lines, axis=0)
     high = whole.astype(jnp.bfloat16)
-    low = (whole - high.astype(jnp.float32)).astype(jnp.bfloat16)
+    return high, (whole - high.astype(jnp.float32)).astype(jnp.bfloat16)
+
+
+def turn_dot(high, low, turn_high_ref, turn_low_ref):
     return (
         jnp.dot(high, turn_high_ref[...], preferred_element_type=jnp.float32)
         + jnp.dot(low, turn_high_ref[...], preferred_element_type=jnp.float32)
@@ -193,11 +204,11 @@
 
 
 def deposit_kernel(across, fields, code_ref, head_ref, turn_high_ref, turn_low_ref, out_ref, tiles):
-    land_tiles(across, fields, pl.program_id(0), code_ref, head_ref, tiles)
+    land_tiles(across, fields, pl.program_id(0), code_ref, head_ref[...].astype(jnp.int32)[:, :across], tiles)
     per = LANES // TE
 
     def one_row(ly, carry):
-        turned = turn_row(across, ly, tiles, turn_high_ref, turn_low_ref)
+        turned = turn_dot(*tile_rows(across, ly, tiles), turn_high_ref, turn_low_ref)
         for c in range(AREA // LANES):
             for a in range(per):
                 out_ref[0, ly * TE + c * per + a] = turned[c * across : (c + 1) * across, a * LANES : (a + 1) * LANES]
@@ -207,38 +218,50 @@
 
 
 def exchange_kernel(
-    across, down, planes, sums_ref, dest_ref, place_ref, count_ref, turn_high_ref, turn_low_ref,
-    mid_ref, above_ref, below_ref, picked, smoothed, head, send, send_head, got, got_head, tiles, halo,
-    send_sem, recv_sem, own_sem, halo_send_sem, halo_recv_sem,
+    across, down, planes, sums_hbm, dest_ref, place_ref, count_ref, turn_high_hbm, turn_low_hbm, out_hbm,
+    sums, turn_high, turn_low, picked, smoothed, head, send, send_head, got, got_head, tiles, line_high, line_low,
+    mid, halo, turned, result, in_sem, out_sem, send_sem, recv_sem, own_sem, halo_send_sem, halo_recv_sem,
 ):
-    fields = sums_ref.shape[0]
+    fields = sums.shape[0]
     peers = across * down
-    height = mid_ref.shape[1]
+    height = mid.shape[1]
     my_x, my_y = lax.axis_index("gx"), lax.axis_index("gy")
     me = my_x * down + my_y
+    mesh_ids = pl.DeviceIdType.MESH
+
+    def load(f):
+        return pltpu.make_async_copy(sums_hbm.at[f], sums.at[f], in_sem.at[f])
+
+    for f in range(fields):
+        load(f).start()
+    load_high = pltpu.make_async_copy(turn_high_hbm, turn_high, in_sem.at[fields])
+    load_low = pltpu.make_async_copy(turn_low_hbm, turn_low, in_sem.at[fields + 1])
+    load_high.start()
+    load_low.start()
 
     barrier = pltpu.get_barrier_semaphore()
 
     def greet(j, carry):
         peer = (me + j) % peers
-        pl.semaphore_signal(
-            barrier, inc=1, device_id=(peer // down, peer % down), device_id_type=pl.DeviceIdType.MESH
-        )
+        pl.semaphore_signal(barrier, inc=1, device_id=(peer // down, peer % down), device_id_type=mesh_ids)
         return carry
 
     lax.fori_loop(1, peers, greet, 0)
+
+    def push(source, target, sem, x, y):
+        pltpu.make_async_remote_copy(
+            src_ref=source.at[x * down + y],
+            dst_ref=target.at[me],
+            send_sem=send_sem.at[sem],
+            recv_sem=recv_sem.at[sem],
+            device_id=(x, y),
+            device_id_type=mesh_ids,
+        ).start()
 
     def post(source, target, sem):
         def one(j, carry):
-            peer = (me + j) % peers
-            pltpu.make_async_remote_copy(
-                src_ref=source.at[peer],
-                dst_ref=target.at[me],
-                send_sem=send_sem.at[sem],
-                recv_sem=recv_sem.at[sem],
-                device_id=(peer // down, peer % down),
-                device_id_type=pl.DeviceIdType.MESH,
-            ).start()
+            peer = (me + 13 * j) % peers
+            push(source, target, sem, peer // down, peer % down)
             return carry
 
         lax.fori_loop(1, peers, one, 0)
@@ -250,21 +273,43 @@
         pltpu.make_async_copy(source.at[rest], target.at[rest], recv_sem.at[sem]).wait()
         pltpu.make_async_copy(source.at[me], target.at[me], own_sem.at[sem]).wait()
 
+    @pl.when(my_y == 0)
+    def _():
+        halo[0] = jnp.zeros(halo.shape[1:], jnp.float32)
+
+    @pl.when(my_y == down - 1)
+    def _():
+        halo[1] = jnp.zeros(halo.shape[1:], jnp.float32)
+
     pick = encode_start(across, down, planes, fields, dest_ref, place_ref, count_ref, head)
 
     def put(f, where, code):
         send[f, where] = code
 
+    def post_column(column):
+        def one(j, carry):
+            x = (my_x + 3 * j + 4) % across
+
+            @pl.when((x != my_x) | (column != my_y))
+            def _():
+                push(send.at[0], got.at[0], 0, x, column)
+
+            return carry
+
+        lax.fori_loop(0, across, one, 0)
+
     def encode(f, carry):
-        encode_field(across, down, planes, f, pick, sums_ref, picked, smoothed, head, put)
-        return carry
-
-    encode(0, 0)
+        load(f).wait()
+        encode_field(across, down, planes, f, pick, sums, picked, smoothed, head, put)
+        return carry
+
+    load(0).wait()
     pl.semaphore_wait(barrier, peers - 1)
-    post(send.at[0], got.at[0], 0)
+    encode_field(across, down, planes, 0, pick, sums, picked, smoothed, head, put, my_y, post_column)
+    pltpu.make_async_copy(send.at[0, me], got.at[0, me], own_sem.at[0]).start()
     lax.fori_loop(1, fields, encode, 0)
     for d in range(peers):
-        send_head[d] = full_head(across, head[d])
+        send_head[d] = jnp.sum(head[d], axis=0, keepdims=True)
     post(send_head, got_head, fields)
 
     def post_field(f, carry):
@@ -275,41 +320,64 @@
 
     def to_before(f):
         return pltpu.make_async_remote_copy(
-            src_ref=mid_ref.at[f, pl.ds(0, RADIUS)],
+            src_ref=mid.at[f, pl.ds(0, RADIUS)],
             dst_ref=halo.at[1, f],
             send_sem=halo_send_sem.at[1, f],
             recv_sem=halo_recv_sem.at[1, f],
             device_id=(my_x, my_y - 1),
-            device_id_type=pl.DeviceIdType.MESH,
+            device_id_type=mesh_ids,
         )
 
     def to_after(f):
         return pltpu.make_async_remote_copy(
-            src_ref=mid_ref.at[f, pl.ds(height - RADIUS, RADIUS)],
+            src_ref=mid.at[f, pl.ds(height - RADIUS, RADIUS)],
             dst_ref=halo.at[0, f],
             send_sem=halo_send_sem.at[0, f],
             recv_sem=halo_recv_sem.at[0, f],
             device_id=(my_x, my_y + 1),
-            device_id_type=pl.DeviceIdType.MESH,
+            device_id_type=mesh_ids,
         )
 
+    load_high.wait()
+    load_low.wait()
     arrived(send_head, got_head, fields)
     per = LANES // TE
+    chunks = AREA // LANES
+    block = chunks * across
+    step = 8
+
+    def write(f, y, values):
+        base = pl.multiple_of(y * across, step * across)
+        for k, value in enumerate(filter_list(values, -RADIUS, step)):
+            turned[pl.ds(base + k * across, across), :] = value
+        for g in range(across):
+            result[f, 0, pl.ds(pl.multiple_of(y, step), step), g * LANES : (g + 1) * LANES] = turned[
+                pl.ds(base + g, step, stride=across), :
+            ]
+
+    def store(f):
+        return pltpu.make_async_copy(result.at[f], out_hbm.at[f], out_sem.at[f])
 
     def deposit(f, carry):
         arrived(send.at[f], got.at[f], f)
-        land_tiles(across, fields, f, got.at[f], got_head, tiles)
-
-        def one_row(ly, inner):
-            turned = turn_row(across, ly, tiles, turn_high_ref, turn_low_ref)
-            for c in range(AREA // LANES):
-                for a in range(per):
-                    mid_ref[f, ly * TE + c * per + a] = turned[
-                        c * across : (c + 1) * across, a * LANES : (a + 1) * LANES
-                    ]
-            return inner
-
-        lax.fori_loop(0, BY, one_row, 0)
+        heads = jnp.broadcast_to(got_head[...], (peers, across, LANES))
+        land_tiles(across, fields, f, got.at[f], heads, tiles)
+
+        for ly in range(BY):
+            line_high[ly * block : (ly + 1) * block], line_low[ly * block : (ly + 1) * block] = tile_rows(
+                across, ly, tiles
+            )
+        span = 2 * LANES
+        for half in range(per * LANES // span):
+            columns = slice(half * span, (half + 1) * span)
+            lines = turn_dot(line_high[...], line_low[...], turn_high.at[:, columns], turn_low.at[:, columns])
+            for ly in range(BY):
+                for c in range(chunks):
+                    for a in range(span // LANES):
+                        row = ly * block + c * across
+                        mid[f, ly * TE + c * per + half * (span // LANES) + a] = lines[
+                            row : row + across, a * LANES : (a + 1) * LANES
+                        ]
 
         @pl.when(my_y > 0)
         def _():
@@ -319,37 +387,35 @@
         def _():
             to_after(f).start()
 
-        return carry
-
-    lax.fori_loop(0, fields, deposit, 0)
-
-    @pl.when(my_y > 0)
-    def _():
-        def one(f, carry):
+        def inner(i, unused):
+            write(f, i * step, [mid[f, i * step - RADIUS + r] for r in range(step + 2 * RADIUS)])
+            return unused
+
+        lax.fori_loop(1, height // step - 1, inner, 0)
+
+        @pl.when(my_y > 0)
+        def _():
             to_before(f).wait_send()
             to_after(f).wait_recv()
-            return carry
-
-        lax.fori_loop(0, fields, one, 0)
-        above_ref[...] = halo[0]
-
-    @pl.when(my_y == 0)
-    def _():
-        above_ref[...] = jnp.zeros_like(above_ref)
-
-    @pl.when(my_y < down - 1)
-    def _():
-        def one(f, carry):
+
+        @pl.when(my_y < down - 1)
+        def _():
             to_after(f).wait_send()
             to_before(f).wait_recv()
-            return carry
-
-        lax.fori_loop(0, fields, one, 0)
-        below_ref[...] = halo[1]
-
-    @pl.when(my_y == down - 1)
-    def _():
-        below_ref[...] = jnp.zeros_like(below_ref)
+
+        write(f, 0, [halo[0, f, r] for r in range(RADIUS)] + [mid[f, r] for r in range(step + RADIUS)])
+        last = height - step - RADIUS
+        write(
+            f,
+            height - step,
+            [mid[f, last + r] for r in range(step + RADIUS)] + [halo[1, f, r] for r in range(RADIUS)],
+        )
+        store(f).start()
+        return carry
+
+    lax.fori_loop(0, fields, deposit, 0)
+    for f in range(fields):
+        store(f).wait()
 
 
 def finish_kernel(across, mid_ref, above_ref, below_ref, out_ref, turned):
@@ -372,30 +438,40 @@
             ]
 
 
-def by_exchange(across, down, planes, fields, operands):
+def by_exchange(across, down, planes, operands):
+    fields, slots, cells = operands[0].shape
     peers = across * down
     width = AREA * across // ROWS
     height = BY * TE
+    lines = BY * (AREA // LANES) * across
+    tables = turn_matrix()
     vmem = pl.BlockSpec(memory_space=pltpu.VMEM)
+    hbm = pl.BlockSpec(memory_space=pl.ANY)
     return pl.pallas_call(
         functools.partial(exchange_kernel, across, down, planes),
-        out_shape=[
-            jax.ShapeDtypeStruct((fields, height, across, LANES), jnp.float32),
-            jax.ShapeDtypeStruct((fields, RADIUS, across, LANES), jnp.float32),
-            jax.ShapeDtypeStruct((fields, RADIUS, across, LANES), jnp.float32),
-        ],
-        in_specs=[vmem] * 6,
-        out_specs=[vmem] * 3,
+        out_shape=jax.ShapeDtypeStruct((fields, 1, height, across * LANES), jnp.float32),
+        in_specs=[hbm, vmem, vmem, vmem, hbm, hbm],
+        out_specs=hbm,
         scratch_shapes=[
+            pltpu.VMEM((fields, slots, cells), jnp.bfloat16),
+            pltpu.VMEM(tables[0].shape, jnp.bfloat16),
+            pltpu.VMEM(tables[1].shape, jnp.bfloat16),
             pltpu.VMEM((peers, planes * AREA), jnp.float32),
             pltpu.VMEM((planes, across, AREA), jnp.float32),
             pltpu.VMEM((peers, across, LANES), jnp.int32),
             pltpu.VMEM((fields, peers, ROWS, width), jnp.int16),
-            pltpu.VMEM((peers, ROWS, LANES), jnp.int16),
+            pltpu.VMEM((peers, 1, LANES), jnp.int32),
             pltpu.VMEM((fields, peers, ROWS, width), jnp.int16),
-            pltpu.VMEM((peers, ROWS, LANES), jnp.int16),
+            pltpu.VMEM((peers, 1, LANES), jnp.int32),
             pltpu.VMEM((TILES * across, AREA), jnp.float32),
+            pltpu.VMEM((lines, tables[0].shape[0]), jnp.bfloat16),
+            pltpu.VMEM((lines, tables[0].shape[0]), jnp.bfloat16),
+            pltpu.VMEM((fields, height, across, LANES), jnp.float32),
             pltpu.VMEM((2, fields, RADIUS, across, LANES), jnp.float32),
+            pltpu.VMEM((height * across, LANES), jnp.float32),
+            pltpu.VMEM((fields, 1, height, across * LANES), jnp.float32),
+            pltpu.SemaphoreType.DMA((fields + 2,)),
+            pltpu.SemaphoreType.DMA((fields,)),
             pltpu.SemaphoreType.DMA((fields + 1,)),
             pltpu.SemaphoreType.DMA((fields + 1,)),
             pltpu.SemaphoreType.DMA((fields + 1,)),
@@ -405,7 +481,7 @@
         compiler_params=pltpu.CompilerParams(
             vmem_limit_bytes=VMEM_BYTES, collective_id=0, has_side_effects=True
         ),
-    )(*operands, *turn_matrix())
+    )(*operands, *tables)
 
 
 def by_all_to_all(across, down, planes, fields, operands):
@@ -457,9 +533,9 @@
         tile_place.reshape(1, slots),
         tile_count.reshape(1, 1),
     )
-    fits = 8 * fields * slots * cells < VMEM_BYTES
-    plan = by_exchange if fits else by_all_to_all
-    mid, above, below = plan(across, down, planes, fields, operands)
+    if 8 * fields * slots * cells < VMEM_BYTES:
+        return by_exchange(across, down, planes, operands)
+    mid, above, below = by_all_to_all(across, down, planes, fields, operands)
     edge = pl.BlockSpec((1, RADIUS, across, LANES), lambda f: (f, 0, 0, 0))
     return pl.pallas_call(
         functools.partial(finish_kernel, across),

time: 80.9 us -> 75.2 us (0.930)
  the two profiles are of different devices: /device:TPU:13 before, /device:TPU:1 now
where the time goes in v4:
time: 75.2 us; the launch traced here: 75.1 us
  Pallas kernels  70.8 us (94%)
  local copies, waits for them, and re-layouts  3.56 us (5%)
    pallas_call x1, Pallas kernels, by_exchange(): pl.pallas_call(functools.partial(exchange_kernel, across, down, planes),...  70.8 us
    unnamed x1, local copies, waits for them, and re-layouts  3.56 us

profile of v4, /device:TPU:1, one launch (start us, length us, event | category | flops | bytes accessed | tf_op | source)
XLA Modules:
  0.0 75.1 jit_solution(11409683403534192021)
XLA Ops:
  0.7 70.8 %shard_map.64 = f32[5,1,128,1024]{3,2,1,0:T(8,128)} custom-call(bf16[5,32,8192]{2,1,0:T(8,128)(2,1)} %bitcast.5, s32[1,32]{1,0:T(1,128)} %bitcast.6, s32[1,32]{1,0:T(1,128)} %bitcast.7, s32[1,1]{1,0:T(1,128)} %bitcast.4.count_ref, bf16[640,512]{1,0:T(8,128)(2,1)} %constant.4.clone.turn_high_hbm, bf16[640,512]{1,0:T(8,128)(2,1)} %constant.5.clone.turn_low_hbm), custom_call_target="tpu_custom_call" | custom-call | tf_op jit(solution)/shard_map/pallas_call | solution.py:450
  71.5 3.6 %copy.9 = f32[5,1,128,1024]{3,2,1,0:T(8,128)} copy(f32[5,1,128,1024]{3,2,1,0:T(8,128)} %shard_map.64) | data formatting | bytes 5242880

commit v5 on v4

--- a/solution.py
+++ b/solution.py
@@ -153,7 +153,7 @@
     return high, low
 
 
-def land_tiles(across, fields, f, code_ref, head, tiles):
+def land_tiles(across, fields, f, code_ref, head, tiles, wait=None):
     sources = code_ref.shape[0]
     parts = ROWS // across
     width = AREA // parts
@@ -167,6 +167,8 @@
     hit = place * across + row % across == column
     low_land = jnp.where(hit, scale, 0.0).T.astype(jnp.bfloat16)
     high_land = (low_land.astype(jnp.float32) * 256.0).astype(jnp.bfloat16)
+    if wait is not None:
+        wait()
     for p in range(parts):
         code = code_ref[...].astype(jnp.int32).reshape(sources, parts, across, width)[:, p]
         code = code.reshape(records, width)
@@ -218,9 +220,9 @@
 
 
 def exchange_kernel(
-    across, down, planes, sums_hbm, dest_ref, place_ref, count_ref, turn_high_hbm, turn_low_hbm, out_hbm,
+    across, down, planes, sums_hbm, dest_ref, place_ref, count_ref, turn_high_hbm, turn_low_hbm, result,
     sums, turn_high, turn_low, picked, smoothed, head, send, send_head, got, got_head, tiles, line_high, line_low,
-    mid, halo, turned, result, in_sem, out_sem, send_sem, recv_sem, own_sem, halo_send_sem, halo_recv_sem,
+    mid, halo, turned, in_sem, send_sem, recv_sem, own_sem, halo_send_sem, halo_recv_sem,
 ):
     fields = sums.shape[0]
     peers = across * down
@@ -355,13 +357,9 @@
                 pl.ds(base + g, step, stride=across), :
             ]
 
-    def store(f):
-        return pltpu.make_async_copy(result.at[f], out_hbm.at[f], out_sem.at[f])
-
     def deposit(f, carry):
-        arrived(send.at[f], got.at[f], f)
         heads = jnp.broadcast_to(got_head[...], (peers, across, LANES))
-        land_tiles(across, fields, f, got.at[f], heads, tiles)
+        land_tiles(across, fields, f, got.at[f], heads, tiles, lambda: arrived(send.at[f], got.at[f], f))
 
         for ly in range(BY):
             line_high[ly * block : (ly + 1) * block], line_low[ly * block : (ly + 1) * block] = tile_rows(
@@ -410,12 +408,9 @@
             height - step,
             [mid[f, last + r] for r in range(step + RADIUS)] + [halo[1, f, r] for r in range(RADIUS)],
         )
-        store(f).start()
         return carry
 
     lax.fori_loop(0, fields, deposit, 0)
-    for f in range(fields):
-        store(f).wait()
 
 
 def finish_kernel(across, mid_ref, above_ref, below_ref, out_ref, turned):
@@ -449,9 +444,9 @@
     hbm = pl.BlockSpec(memory_space=pl.ANY)
     return pl.pallas_call(
         functools.partial(exchange_kernel, across, down, planes),
-        out_shape=jax.ShapeDtypeStruct((fields, 1, height, across * LANES), jnp.float32),
+        out_shape=pltpu.VMEM((fields, 1, height, across * LANES), jnp.float32),
         in_specs=[hbm, vmem, vmem, vmem, hbm, hbm],
-        out_specs=hbm,
+        out_specs=vmem,
         scratch_shapes=[
             pltpu.VMEM((fields, slots, cells), jnp.bfloat16),
             pltpu.VMEM(tables[0].shape, jnp.bfloat16),
@@ -469,9 +464,7 @@
             pltpu.VMEM((fields, height, across, LANES), jnp.float32),
             pltpu.VMEM((2, fields, RADIUS, across, LANES), jnp.float32),
             pltpu.VMEM((height * across, LANES), jnp.float32),
-            pltpu.VMEM((fields, 1, height, across * LANES), jnp.float32),
             pltpu.SemaphoreType.DMA((fields + 2,)),
-            pltpu.SemaphoreType.DMA((fields,)),
             pltpu.SemaphoreType.DMA((fields + 1,)),
             pltpu.SemaphoreType.DMA((fields + 1,)),
             pltpu.SemaphoreType.DMA((fields + 1,)),
@@ -479,7 +472,7 @@
             pltpu.SemaphoreType.DMA((2, fields)),
         ],
         compiler_params=pltpu.CompilerParams(
-            vmem_limit_bytes=VMEM_BYTES, collective_id=0, has_side_effects=True
+            vmem_limit_bytes=VMEM_BYTES // 2, collective_id=0, has_side_effects=True
         ),
     )(*operands, *tables)
 
@@ -533,7 +526,7 @@
         tile_place.reshape(1, slots),
         tile_count.reshape(1, 1),
     )
-    if 8 * fields * slots * cells < VMEM_BYTES:
+    if 16 * fields * slots * cells < VMEM_BYTES:
         return by_exchange(across, down, planes, operands)
     mid, above, below = by_all_to_all(across, down, planes, fields, operands)
     edge = pl.BlockSpec((1, RADIUS, across, LANES), lambda f: (f, 0, 0, 0))

time: 75.2 us -> 77.6 us (1.032)
  local copies, waits for them, and re-layouts: 3.56 us -> 6.71 us
  Pallas kernels: 70.8 us -> 69.9 us
    unnamed x1 -> x11, local copies, waits for them, and re-layouts: 3.56 us -> 6.71 us
    pallas_call x1, Pallas kernels: 70.8 us -> 69.9 us  [by_exchange(): pl.pallas_call(functools.partial(exchange_kernel, across, down, planes),...]
where the time goes in v5:
time: 77.6 us; the launch traced here: 77.3 us
  Pallas kernels  69.9 us (90%)
  local copies, waits for them, and re-layouts  6.71 us (9%)
    pallas_call x1, Pallas kernels, by_exchange(): pl.pallas_call(functools.partial(exchange_kernel, across, down, planes),...  69.9 us
    unnamed x11, local copies, waits for them, and re-layouts  6.71 us

profile of v5, /device:TPU:1, one launch (start us, length us, event | category | flops | bytes accessed | tf_op | source)
XLA Modules:
  0.0 77.3 jit_solution(9258056968351330818)
XLA Ops:
  0.7 0.0 copy-start
  0.7 1.7 %copy-done = bf16[32,5,8192]{2,0,1:T(8,128)(2,1)S(1)} copy-done((bf16[32,5,8192]{2,0,1:T(8,128)(2,1)S(1)}, bf16[32,5,8192]{2,0,1:T(8,128)(2,1)}, u32[]{:S(2)}) %copy-start) | copy-done | bytes 2621464
  2.4 0.0 copy-start.1
  2.4 1.1 %copy-done.1 = bf16[640,512]{1,0:T(8,128)(2,1)S(1)} copy-done((bf16[640,512]{1,0:T(8,128)(2,1)S(1)}, bf16[640,512]{1,0:T(8,128)(2,1)}, u32[]{:S(2)}) %copy-start.1) | copy-done | bytes 655384
  3.5 0.0 copy-start.2
  3.5 1.1 %copy-done.2 = bf16[640,512]{1,0:T(8,128)(2,1)S(1)} copy-done((bf16[640,512]{1,0:T(8,128)(2,1)S(1)}, bf16[640,512]{1,0:T(8,128)(2,1)}, u32[]{:S(2)}) %copy-start.2) | copy-done | bytes 655384
  4.6 0.0 copy-start.3
  4.6 0.7 copy-done.3
  5.2 0.0 copy-start.4
  5.2 0.7 copy-done.4
  5.9 69.9 %shard_map.64 = f32[5,1,128,1024]{3,2,1,0:T(8,128)S(1)} custom-call(bf16[5,32,8192]{2,1,0:T(8,128)(2,1)S(1)} %bitcast.5, s32[1,32]{1,0:T(1,128)S(1)} %bitcast.6, s32[1,32]{1,0:T(1,128)S(1)} %bitcast.7, s32[1,1]{1,0:T(1,128)} %bitcast.4.count_ref, bf16[640,512]{1,0:T(8,128)(2,1)S(1)} %copy-done.2, bf16[640,512]{1,0:T(8,128)(2,1)S(1)} %copy-done.1), custom_call_target="tpu_custom_call" | custom-call | tf_op jit(solution)/shard_map/pallas_call | solution.py:445
  75.8 1.5 %copy.8 = f32[5,1,128,1024]{3,2,1,0:T(8,128)} copy(f32[5,1,128,1024]{3,2,1,0:T(8,128)S(1)} %shard_map.64) | data formatting | bytes 5242880
Async XLA Ops:
  0.7 1.7 %copy-start = (bf16[32,5,8192]{2,0,1:T(8,128)(2,1)S(1)}, bf16[32,5,8192]{2,0,1:T(8,128)(2,1)}, u32[]{:S(2)}) copy-start(bf16[32,5,8192]{2,0,1:T(8,128)(2,1)} %param.6) | copy-start | bytes 7864324
  2.4 1.1 %copy-start.1 = (bf16[640,512]{1,0:T(8,128)(2,1)S(1)}, bf16[640,512]{1,0:T(8,128)(2,1)}, u32[]{:S(2)}) copy-start(bf16[640,512]{1,0:T(8,128)(2,1)} %constant.5.clone.turn_low_hbm) | copy-start | bytes 1966084
  3.5 1.1 %copy-start.2 = (bf16[640,512]{1,0:T(8,128)(2,1)S(1)}, bf16[640,512]{1,0:T(8,128)(2,1)}, u32[]{:S(2)}) copy-start(bf16[640,512]{1,0:T(8,128)(2,1)} %constant.4.clone.turn_high_hbm) | copy-start | bytes 1966084
  4.6 0.7 copy-start.3
  5.2 0.7 copy-start.4

commit v6 on v5

--- a/solution.py
+++ b/solution.py
@@ -72,13 +72,16 @@
     return jnp.where(chosen, 1.0, 0.0).astype(jnp.bfloat16)
 
 
-def encode_field(across, down, planes, f, pick, sums_ref, picked, smoothed, head, put, first=0, after=None):
+def encode_field(across, down, planes, f, pick, sums_ref, picked, smoothed, head, put, first=0, ready=None, after=None):
     parts = ROWS // across
     width = AREA // parts
     spot = head_spot(across)
     for z in range(planes):
         span = slice(z * AREA, (z + 1) * AREA)
         picked[:, span] = jnp.dot(pick, sums_ref[f, :, span], preferred_element_type=jnp.float32)
+
+    if ready is not None:
+        ready()
 
     def one_column(index, carry):
         column = (index + first) % down
@@ -220,8 +223,8 @@
 
 
 def exchange_kernel(
-    across, down, planes, sums_hbm, dest_ref, place_ref, count_ref, turn_high_hbm, turn_low_hbm, result,
-    sums, turn_high, turn_low, picked, smoothed, head, send, send_head, got, got_head, tiles, line_high, line_low,
+    across, down, planes, sums_hbm, dest_hbm, place_hbm, count_ref, turn_high_hbm, turn_low_hbm, result,
+    sums, dest_ref, place_ref, turn_high, turn_low, picked, smoothed, head, send, send_head, got, got_head, tiles, line_high, line_low,
     mid, halo, turned, in_sem, send_sem, recv_sem, own_sem, halo_send_sem, halo_recv_sem,
 ):
     fields = sums.shape[0]
@@ -234,6 +237,10 @@
     def load(f):
         return pltpu.make_async_copy(sums_hbm.at[f], sums.at[f], in_sem.at[f])
 
+    load_dest = pltpu.make_async_copy(dest_hbm, dest_ref, in_sem.at[fields + 2])
+    load_place = pltpu.make_async_copy(place_hbm, place_ref, in_sem.at[fields + 3])
+    load_dest.start()
+    load_place.start()
     for f in range(fields):
         load(f).start()
     load_high = pltpu.make_async_copy(turn_high_hbm, turn_high, in_sem.at[fields])
@@ -283,6 +290,8 @@
     def _():
         halo[1] = jnp.zeros(halo.shape[1:], jnp.float32)
 
+    load_dest.wait()
+    load_place.wait()
     pick = encode_start(across, down, planes, fields, dest_ref, place_ref, count_ref, head)
 
     def put(f, where, code):
@@ -306,8 +315,8 @@
         return carry
 
     load(0).wait()
-    pl.semaphore_wait(barrier, peers - 1)
-    encode_field(across, down, planes, 0, pick, sums, picked, smoothed, head, put, my_y, post_column)
+    everyone = lambda: pl.semaphore_wait(barrier, peers - 1)
+    encode_field(across, down, planes, 0, pick, sums, picked, smoothed, head, put, my_y, everyone, post_column)
     pltpu.make_async_copy(send.at[0, me], got.at[0, me], own_sem.at[0]).start()
     lax.fori_loop(1, fields, encode, 0)
     for d in range(peers):
@@ -441,14 +450,16 @@
     lines = BY * (AREA // LANES) * across
     tables = turn_matrix()
     vmem = pl.BlockSpec(memory_space=pltpu.VMEM)
-    hbm = pl.BlockSpec(memory_space=pl.ANY)
+    hbm = pl.BlockSpec(memory_space=pltpu.HBM)
     return pl.pallas_call(
         functools.partial(exchange_kernel, across, down, planes),
         out_shape=pltpu.VMEM((fields, 1, height, across * LANES), jnp.float32),
-        in_specs=[hbm, vmem, vmem, vmem, hbm, hbm],
+        in_specs=[hbm, hbm, hbm, vmem, hbm, hbm],
         out_specs=vmem,
         scratch_shapes=[
             pltpu.VMEM((fields, slots, cells), jnp.bfloat16),
+            pltpu.VMEM((1, slots), jnp.int32),
+            pltpu.VMEM((1, slots), jnp.int32),
             pltpu.VMEM(tables[0].shape, jnp.bfloat16),
             pltpu.VMEM(tables[1].shape, jnp.bfloat16),
             pltpu.VMEM((peers, planes * AREA), jnp.float32),
@@ -464,7 +475,7 @@
             pltpu.VMEM((fields, height, across, LANES), jnp.float32),
             pltpu.VMEM((2, fields, RADIUS, across, LANES), jnp.float32),
             pltpu.VMEM((height * across, LANES), jnp.float32),
-            pltpu.SemaphoreType.DMA((fields + 2,)),
+            pltpu.SemaphoreType.DMA((fields + 4,)),
             pltpu.SemaphoreType.DMA((fields + 1,)),
             pltpu.SemaphoreType.DMA((fields + 1,)),
             pltpu.SemaphoreType.DMA((fields + 1,)),
@@ -472,7 +483,7 @@
             pltpu.SemaphoreType.DMA((2, fields)),
         ],
         compiler_params=pltpu.CompilerParams(
-            vmem_limit_bytes=VMEM_BYTES // 2, collective_id=0, has_side_effects=True
+            vmem_limit_bytes=VMEM_BYTES, collective_id=0, has_side_effects=True
         ),
     )(*operands, *tables)
 

time: 77.6 us -> 71.5 us (0.921)
  local copies, waits for them, and re-layouts: 6.71 us -> 1.49 us
  Pallas kernels: 69.9 us -> 69.1 us
    unnamed x11 -> x1, local copies, waits for them, and re-layouts: 6.71 us -> 1.49 us
where the time goes in v6:
time: 71.5 us; the launch traced here: 71.3 us
  Pallas kernels  69.1 us (97%)
  local copies, waits for them, and re-layouts  1.49 us (2%)
    pallas_call x1, Pallas kernels, by_exchange(): pl.pallas_call(functools.partial(exchange_kernel, across, down, planes),...  69.1 us
    unnamed x1, local copies, waits for them, and re-layouts  1.49 us

profile of v6, /device:TPU:1, one launch (start us, length us, event | category | flops | bytes accessed | tf_op | source)
XLA Modules:
  0.0 71.3 jit_solution(15673480010077430383)
XLA Ops:
  0.7 69.1 %shard_map.64 = f32[5,1,128,1024]{3,2,1,0:T(8,128)S(1)} custom-call(bf16[5,32,8192]{2,1,0:T(8,128)(2,1)} %bitcast.5, s32[1,32]{1,0:T(1,128)} %bitcast.6, s32[1,32]{1,0:T(1,128)} %bitcast.7, s32[1,1]{1,0:T(1,128)} %bitcast.4.count_ref, bf16[640,512]{1,0:T(8,128)(2,1)} %constant.4.clone.turn_high_hbm, bf16[640,512]{1,0:T(8,128)(2,1)} %constant.5.clone.turn_low_hbm), custom_call_target="tpu_custom_call" | custom-call | tf_op jit(solution)/shard_map/pallas_call | solution.py:454
  69.8 1.5 %copy.8 = f32[5,1,128,1024]{3,2,1,0:T(8,128)} copy(f32[5,1,128,1024]{3,2,1,0:T(8,128)S(1)} %shard_map.64) | data formatting | bytes 5242880
